TPU v7x, 32 devices: a whole 2x2x4 slice. The times are simulated.
32 devices in a mesh: groups: 2 (over y), gx: 4 (over z), gy: 4 (over x, core).
Axes of the slice: x: 2, y: 2, z: 4, core: 2. Of those that a mesh axis runs over, the one named last changes fastest.
Arguments:
- populations: float32 [19, 64, 64, 128], P(None, ('groups', 'gx'), 'gy'), parts along dimension 1, may hold values from 0 to 1.1, as said below
- fluid_mask: int32 [64, 64, 128], P(('groups', 'gx'), 'gy'), parts along dimension 0, may hold values 0 or 1
- wet_class: int32 [64, 64, 128], P(('groups', 'gx'), 'gy'), parts along dimension 0, may hold values from 0 to 3
- wall_potential: float32 [8], P('groups'), parts along dimension 0, may hold values from 0 to 1
- relax_rates: float32 [19], replicated, may hold values from 0.8 to 1.6
Outputs:
- populations_out: float32 [19, 64, 64, 128], P(None, ('groups', 'gx'), 'gy'), parts along dimension 1
- velocity: float32 [3, 64, 64, 128], P(None, ('groups', 'gx'), 'gy'), parts along dimension 1
There are 2 independent parts, one for each index of `groups`. A program takes and returns all parts, laid end to end along the dimension named above; an argument that names none is the same for every part. Nothing has to cross between parts.
Inputs may be any that keep to these rules, and one draw needn't show every extreme that they name: `populations`: every population is positive.
All inputs are finite; a program needn't handle non-finite values. No bound on the sum of `fluid_mask` on one device may be relied on, other than what follows from the above.
Results may differ from a plain program's by a relative error of at most 0.0003.
Values sent between devices are 32-bit elements; how exact they have to be, the bound alone decides.
A program may use at most 64 MiB of HBM per device.

v0:
```python
import jax
import jax.numpy as jnp
import numpy as np
from jax import lax
from jax.sharding import PartitionSpec as P

WET_CLASSES = 4
STEPS = 4


coupling = -2.5


def extended(cells, sides, width):
    for axis, dim in sides:
        count = lax.axis_size(axis)
        head = lax.slice_in_dim(cells, 0, width, axis=dim)
        tail = lax.slice_in_dim(cells, cells.shape[dim] - width, cells.shape[dim], axis=dim)
        cells = jnp.concatenate(
            [
                lax.ppermute(tail, axis, [(i, (i + 1) % count) for i in range(count)]),
                cells,
                lax.ppermute(head, axis, [((i + 1) % count, i) for i in range(count)]),
            ],
            axis=dim,
        )
    return cells


def lattice():
    velocity_set = np.array(
        [
            [0, 0, 0],
            [1, 0, 0],
            [-1, 0, 0],
            [0, 1, 0],
            [0, -1, 0],
            [0, 0, 1],
            [0, 0, -1],
            [1, 1, 0],
            [-1, -1, 0],
            [1, -1, 0],
            [-1, 1, 0],
            [1, 0, 1],
            [-1, 0, -1],
            [1, 0, -1],
            [-1, 0, 1],
            [0, 1, 1],
            [0, -1, -1],
            [0, 1, -1],
            [0, -1, 1],
        ]
    )
    weights = [1.0 / 3.0] + [1.0 / 18.0] * 6 + [1.0 / 36.0] * 12
    opposite = [0] + [index + 1 if index % 2 == 1 else index - 1 for index in range(1, 19)]
    lattice_vel = jnp.asarray(velocity_set, jnp.float32)
    along_x = lattice_vel[:, 0]
    along_y = lattice_vel[:, 1]
    along_z = lattice_vel[:, 2]
    moment_basis = jnp.stack(
        [
            jnp.ones(19, jnp.float32),
            along_x,
            along_y,
            along_z,
            along_x * along_y,
            along_x * along_z,
            along_y * along_z,
            along_x * along_x,
            along_y * along_y,
            along_z * along_z,
            along_x * along_y * along_y,
            along_x * along_z * along_z,
            along_y * along_x * along_x,
            along_y * along_z * along_z,
            along_z * along_x * along_x,
            along_z * along_y * along_y,
            along_x * along_x * along_y * along_y,
            along_x * along_x * along_z * along_z,
            along_y * along_y * along_z * along_z,
        ]
    )
    return (velocity_set, weights, opposite, moment_basis)


def collide_matrix(moment_basis, relax_rates):
    gram = jnp.dot(moment_basis, moment_basis.T, precision=lax.Precision.HIGHEST)
    factor = jnp.linalg.cholesky(gram)
    scaled = relax_rates[:, None] * moment_basis
    solved = jax.scipy.linalg.cho_solve((factor, True), scaled)
    return jnp.dot(moment_basis.T, solved, precision=lax.Precision.HIGHEST)


def offset_view(padded, step_x, step_y, step_z, rows_x, rows_y):
    window = padded[..., 1 + step_x : 1 + step_x + rows_x, 1 + step_y : 1 + step_y + rows_y, :]
    return jnp.roll(window, -step_z, axis=-1)


def collision(populations, fluid, potential, near_list, collide, velocity_set, weights):
    pull = [jnp.zeros_like(potential), jnp.zeros_like(potential), jnp.zeros_like(potential)]
    for index in range(1, 19):
        for column in range(3):
            if velocity_set[index][column] != 0:
                pull[column] = (
                    pull[column]
                    + float(weights[index] * int(velocity_set[index][column])) * near_list[index]
                )
    force = -coupling * potential[None] * jnp.stack(pull)
    density = jnp.sum(populations, axis=0)
    safe_density = jnp.where(fluid, density, 1.0)
    lattice_vel = jnp.asarray(velocity_set, jnp.float32)
    momentum = jnp.einsum(
        "kc,kxyz->cxyz", lattice_vel, populations, precision=lax.Precision.HIGHEST
    )
    speed = (momentum + 0.5 * force) / safe_density[None]
    along = jnp.einsum("kc,cxyz->kxyz", lattice_vel, speed, precision=lax.Precision.HIGHEST)
    push = jnp.einsum("kc,cxyz->kxyz", lattice_vel, force, precision=lax.Precision.HIGHEST)
    speed_sq = jnp.sum(speed * speed, axis=0)
    speed_force = jnp.sum(speed * force, axis=0)
    weight_col = jnp.asarray(weights, jnp.float32)[:, None, None, None]
    equil = (
        weight_col
        * safe_density[None]
        * (1.0 + 3.0 * along + 4.5 * along * along - 1.5 * speed_sq[None])
    )
    source = weight_col * (3.0 * (push - speed_force[None]) + 9.0 * along * push)
    excess = populations - equil + 0.5 * source
    shape = populations.shape
    relaxed = jnp.dot(
        collide, excess.reshape(shape[0], -1), precision=lax.Precision.HIGHEST
    ).reshape(shape)
    return (populations + source - relaxed, speed)


def per_device(populations, fluid_mask, wet_class, wall_potential, relax_rates):
    velocity_set, weights, opposite, moment_basis = lattice()
    rows_x, rows_y = (fluid_mask.shape[0], fluid_mask.shape[1])
    collide = collide_matrix(moment_basis, relax_rates)
    fluid = fluid_mask == 1
    classes = jnp.arange(WET_CLASSES, dtype=jnp.int32)[:, None, None, None]
    wall_values = jnp.sum(
        jnp.where(wet_class[None] == classes, wall_potential[:, None, None, None], 0.0), axis=0
    )
    shifts = [[int(value) for value in velocity_set[index]] for index in range(19)]
    mask_padded = extended(fluid_mask, (("gx", 0), ("gy", 1)), 1)
    inflow = jnp.stack(
        [
            offset_view(
                mask_padded, -shifts[index][0], -shifts[index][1], -shifts[index][2], rows_x, rows_y
            )
            == 1
            for index in range(19)
        ]
    )
    speed = None
    for step in range(STEPS):
        density = jnp.sum(populations, axis=0)
        safe_density = jnp.where(fluid, density, 1.0)
        potential = jnp.where(fluid, 1.0 - jnp.exp(-safe_density), wall_values)
        pot_padded = extended(potential, (("gx", 0), ("gy", 1)), 1)
        near_list = [None] + [
            offset_view(
                pot_padded, shifts[index][0], shifts[index][1], shifts[index][2], rows_x, rows_y
            )
            for index in range(1, 19)
        ]
        post, speed = collision(
            populations, fluid, potential, near_list, collide, velocity_set, weights
        )
        post_padded = extended(post, (("gx", 1), ("gy", 2)), 1)
        passed = jnp.stack(
            [
                offset_view(
                    post_padded[index],
                    -shifts[index][0],
                    -shifts[index][1],
                    -shifts[index][2],
                    rows_x,
                    rows_y,
                )
                for index in range(19)
            ]
        )
        bounced = jnp.stack([post[opposite[index]] for index in range(19)])
        populations = jnp.where(fluid[None], jnp.where(inflow, passed, bounced), 0.0)
    velocity = jnp.where(fluid[None], speed, 0.0)
    return (populations, velocity)


def solution(mesh):
    return jax.shard_map(
        per_device,
        mesh=mesh,
        in_specs=(
            P(None, ("groups", "gx"), "gy", None),
            P(("groups", "gx"), "gy", None),
            P(("groups", "gx"), "gy", None),
            P("groups"),
            P(),
        ),
        out_specs=(P(None, ("groups", "gx"), "gy", None), P(None, ("groups", "gx"), "gy", None)),
        check_vma=False,
    )
```

profile of v0, /device:TPU:1, one launch (start us, length us, event | category | flops | bytes accessed | tf_op | source)
XLA Modules:
  0.0 164.9 jit_solution(5444248923794930865)
XLA Ops:
  1.4 4.2 %collective-permute-start.1 = (s32[1,16,128]{2,1,0:T(8,128)S(1)}, s32[1,16,128]{2,1,0:T(8,128)S(1)}, u32[]{:S(2)}, u32[]{:S(2)}) collective-permute-start(s32[1,16,128]{2,1,0:T(8,128)S(1)} %get-tuple-element.317), channel_id=1, source_target_pairs={{4,0},{8,4},{12,8},{0,12},{5,1},{9,5},{13,9},{1,13},{6,2},{10,6},{... | collective-permute-start | bytes 24584 | tf_op jit(solution)/shard_map/ppermute | solution.py:23
  7.4 3.3 %collective-permute-start.4 = (f32[1,16,128]{2,1,0:T(8,128)S(1)}, f32[1,16,128]{2,1,0:T(8,128)S(1)}, u32[]{:S(2)}, u32[]{:S(2)}) collective-permute-start(f32[1,16,128]{2,1,0:T(8,128)S(1)} %get-tuple-element.309), channel_id=1, source_target_pairs={{4,0},{8,4},{12,8},{0,12},{5,1},{9,5},{13,9},{1,13},{6,2},{10,6},{... | collective-permute-start | bytes 24584 | tf_op jit(solution)/shard_map/ppermute | solution.py:23
  10.8 2.4 %cholesky.16 = f32[19,19]{1,0:T(8,128)S(1)} custom-call(f32[19,19]{1,0:T(8,128)} %constant.111), custom_call_target="Cholesky" | custom-call | tf_op jit(solution)/shard_map/jit(cholesky)/cholesky | solution.py:88
  19.2 2.7 %collective-permute-start.7 = (f32[10,1,128]{2,1,0:T(1,128)S(1)}, f32[10,1,128]{2,1,0:T(1,128)S(1)}, u32[]{:S(2)}, u32[]{:S(2)}) collective-permute-start(f32[10,1,128]{2,1,0:T(1,128)S(1)} %get-tuple-element.222), channel_id=1, source_target_pairs={{0,1},{1,2},{2,3},{3,0},{4,5},{5,6},{6,7},{7,4},{8,9},{9,10},{10,1... | collective-permute-start | bytes 15368 | tf_op jit(solution)/shard_map/ppermute | solution.py:21
  29.6 2.0 %fusion.12 = f32[19,8,16,128]{3,0,2,1:T(8,128)S(1)} fusion(f32[19,19,1,1]{1,0,3,2:T(8,128)S(1)} %convolution_bitcast_fusion, f32[8,16,128,19]{2,1,0,3:T(8,128)S(1)} %fusion.284), kind=kOutput, calls=%fused_computation.20 | convolution fusion | flops 70975488 | bytes 2491812 | tf_op jit(solution)/shard_map/dot_general | solution.py:129
  32.5 15.0 %collective-permute-start.9 = (f32[19,1,16,128]{3,2,1,0:T(8,128)S(1)}, f32[19,1,16,128]{3,2,1,0:T(8,128)S(1)}, u32[]{:S(2)}, u32[]{:S(2)}) collective-permute-start(f32[19,1,16,128]{3,2,1,0:T(8,128)S(1)} %get-tuple-element.132), channel_id=1, source_target_pairs={{4,0},{8,4},{12,8},{0,12},{5,1},{9,5},{13,9},{1,13},{6,2},{10,6},{... | collective-permute-start | bytes 466952 | tf_op jit(solution)/shard_map/ppermute | solution.py:23
  53.6 2.4 %collective-permute-done.11 = f32[19,10,1,128]{3,2,1,0:T(1,128)S(1)} collective-permute-done((f32[19,10,1,128]{3,2,1,0:T(1,128)S(1)}, f32[19,10,1,128]{3,2,1,0:T(1,128)S(1)}, u32[]{:S(2)}, u32[]{:S(2)}) %collective-permute-start.11) | collective-permute-done | bytes 97312 | tf_op jit(solution)/shard_map/ppermute | solution.py:23
  59.0 4.1 %collective-permute-start.12 = (f32[1,16,128]{2,1,0:T(8,128)S(1)}, f32[1,16,128]{2,1,0:T(8,128)S(1)}, u32[]{:S(2)}, u32[]{:S(2)}) collective-permute-start(f32[1,16,128]{2,1,0:T(8,128)S(1)} %get-tuple-element.299), channel_id=1, source_target_pairs={{4,0},{8,4},{12,8},{0,12},{5,1},{9,5},{13,9},{1,13},{6,2},{10,6},{... | collective-permute-start | bytes 24584 | tf_op jit(solution)/shard_map/ppermute | solution.py:23
  66.0 2.2 %collective-permute-done.14 = f32[10,1,128]{2,1,0:T(1,128)S(1)} collective-permute-done((f32[10,1,128]{2,1,0:T(1,128)S(1)}, f32[10,1,128]{2,1,0:T(1,128)S(1)}, u32[]{:S(2)}, u32[]{:S(2)}) %collective-permute-start.14) | collective-permute-done | bytes 5152 | tf_op jit(solution)/shard_map/ppermute | solution.py:23
  76.6 2.8 %collective-permute-start.17 = (f32[19,1,16,128]{3,2,1,0:T(8,128)S(1)}, f32[19,1,16,128]{3,2,1,0:T(8,128)S(1)}, u32[]{:S(2)}, u32[]{:S(2)}) collective-permute-start(f32[19,1,16,128]{3,2,1,0:T(8,128)S(1)} %get-tuple-element.130), channel_id=1, source_target_pairs={{4,0},{8,4},{12,8},{0,12},{5,1},{9,5},{13,9},{1,13},{6,2},{10,6},{... | collective-permute-start | bytes 466952 | tf_op jit(solution)/shard_map/ppermute | solution.py:23
  79.7 4.0 %collective-permute-done.16 = f32[19,1,16,128]{3,2,1,0:T(8,128)S(1)} collective-permute-done((f32[19,1,16,128]{3,2,1,0:T(8,128)S(1)}, f32[19,1,16,128]{3,2,1,0:T(8,128)S(1)}, u32[]{:S(2)}, u32[]{:S(2)}) %collective-permute-start.16) | collective-permute-done | bytes 155680 | tf_op jit(solution)/shard_map/ppermute | solution.py:21
  83.7 2.1 %collective-permute-done.17 = f32[19,1,16,128]{3,2,1,0:T(8,128)S(1)} collective-permute-done((f32[19,1,16,128]{3,2,1,0:T(8,128)S(1)}, f32[19,1,16,128]{3,2,1,0:T(8,128)S(1)}, u32[]{:S(2)}, u32[]{:S(2)}) %collective-permute-start.17) | collective-permute-done | bytes 155680 | tf_op jit(solution)/shard_map/ppermute | solution.py:23
  88.9 2.4 %collective-permute-done.19 = f32[19,10,1,128]{3,2,1,0:T(1,128)S(1)} collective-permute-done((f32[19,10,1,128]{3,2,1,0:T(1,128)S(1)}, f32[19,10,1,128]{3,2,1,0:T(1,128)S(1)}, u32[]{:S(2)}, u32[]{:S(2)}) %collective-permute-start.19) | collective-permute-done | bytes 97312 | tf_op jit(solution)/shard_map/ppermute | solution.py:23
  95.4 2.2 %collective-permute-start.20 = (f32[1,16,128]{2,1,0:T(8,128)S(1)}, f32[1,16,128]{2,1,0:T(8,128)S(1)}, u32[]{:S(2)}, u32[]{:S(2)}) collective-permute-start(f32[1,16,128]{2,1,0:T(8,128)S(1)} %get-tuple-element.289), channel_id=1, source_target_pairs={{4,0},{8,4},{12,8},{0,12},{5,1},{9,5},{13,9},{1,13},{6,2},{10,6},{... | collective-permute-start | bytes 24584 | tf_op jit(solution)/shard_map/ppermute | solution.py:23
  100.7 2.7 %collective-permute-done.22 = f32[10,1,128]{2,1,0:T(1,128)S(1)} collective-permute-done((f32[10,1,128]{2,1,0:T(1,128)S(1)}, f32[10,1,128]{2,1,0:T(1,128)S(1)}, u32[]{:S(2)}, u32[]{:S(2)}) %collective-permute-start.22) | collective-permute-done | bytes 5152 | tf_op jit(solution)/shard_map/ppermute | solution.py:23
  111.1 3.6 %collective-permute-start.25 = (f32[19,1,16,128]{3,2,1,0:T(8,128)S(1)}, f32[19,1,16,128]{3,2,1,0:T(8,128)S(1)}, u32[]{:S(2)}, u32[]{:S(2)}) collective-permute-start(f32[19,1,16,128]{3,2,1,0:T(8,128)S(1)} %get-tuple-element.128), channel_id=1, source_target_pairs={{4,0},{8,4},{12,8},{0,12},{5,1},{9,5},{13,9},{1,13},{6,2},{10,6},{... | collective-permute-start | bytes 466952 | tf_op jit(solution)/shard_map/ppermute | solution.py:23
  114.9 4.0 %collective-permute-done.24 = f32[19,1,16,128]{3,2,1,0:T(8,128)S(1)} collective-permute-done((f32[19,1,16,128]{3,2,1,0:T(8,128)S(1)}, f32[19,1,16,128]{3,2,1,0:T(8,128)S(1)}, u32[]{:S(2)}, u32[]{:S(2)}) %collective-permute-start.24) | collective-permute-done | bytes 155680 | tf_op jit(solution)/shard_map/ppermute | solution.py:21
  122.9 2.4 %collective-permute-done.27 = f32[19,10,1,128]{3,2,1,0:T(1,128)S(1)} collective-permute-done((f32[19,10,1,128]{3,2,1,0:T(1,128)S(1)}, f32[19,10,1,128]{3,2,1,0:T(1,128)S(1)}, u32[]{:S(2)}, u32[]{:S(2)}) %collective-permute-start.27) | collective-permute-done | bytes 97312 | tf_op jit(solution)/shard_map/ppermute | solution.py:23
  128.3 2.3 %collective-permute-start.29 = (f32[1,16,128]{2,1,0:T(8,128)S(1)}, f32[1,16,128]{2,1,0:T(8,128)S(1)}, u32[]{:S(2)}, u32[]{:S(2)}) collective-permute-start(f32[1,16,128]{2,1,0:T(8,128)S(1)} %get-tuple-element.278), channel_id=1, source_target_pairs={{0,4},{4,8},{8,12},{12,0},{1,5},{5,9},{9,13},{13,1},{2,6},{6,10},{... | collective-permute-start | bytes 24584 | tf_op jit(solution)/shard_map/ppermute | solution.py:21
  135.7 2.3 %collective-permute-done.30 = f32[10,1,128]{2,1,0:T(1,128)S(1)} collective-permute-done((f32[10,1,128]{2,1,0:T(1,128)S(1)}, f32[10,1,128]{2,1,0:T(1,128)S(1)}, u32[]{:S(2)}, u32[]{:S(2)}) %collective-permute-start.30) | collective-permute-done | bytes 5152 | tf_op jit(solution)/shard_map/ppermute | solution.py:23
  143.5 2.0 %fusion = f32[19,8,16,128]{3,0,2,1:T(8,128)S(1)} fusion(f32[19,19,1,1]{1,0,3,2:T(8,128)S(1)} %convolution_bitcast_fusion, f32[8,16,128,19]{2,1,0,3:T(8,128)S(1)} %fusion.281), kind=kOutput, calls=%fused_computation.8 | convolution fusion | flops 70975488 | bytes 2491812 | tf_op jit(solution)/shard_map/dot_general | solution.py:129
  147.2 2.4 %collective-permute-start.33 = (f32[19,1,16,128]{3,2,1,0:T(8,128)S(1)}, f32[19,1,16,128]{3,2,1,0:T(8,128)S(1)}, u32[]{:S(2)}, u32[]{:S(2)}) collective-permute-start(f32[19,1,16,128]{3,2,1,0:T(8,128)S(1)} %get-tuple-element.126), channel_id=1, source_target_pairs={{4,0},{8,4},{12,8},{0,12},{5,1},{9,5},{13,9},{1,13},{6,2},{10,6},{... | collective-permute-start | bytes 466952 | tf_op jit(solution)/shard_map/ppermute | solution.py:23
  149.8 4.0 %collective-permute-done.32 = f32[19,1,16,128]{3,2,1,0:T(8,128)S(1)} collective-permute-done((f32[19,1,16,128]{3,2,1,0:T(8,128)S(1)}, f32[19,1,16,128]{3,2,1,0:T(8,128)S(1)}, u32[]{:S(2)}, u32[]{:S(2)}) %collective-permute-start.32) | collective-permute-done | bytes 155680 | tf_op jit(solution)/shard_map/ppermute | solution.py:21
  156.8 2.2 %collective-permute-done.34 = f32[19,10,1,128]{3,2,1,0:T(1,128)S(1)} collective-permute-done((f32[19,10,1,128]{3,2,1,0:T(1,128)S(1)}, f32[19,10,1,128]{3,2,1,0:T(1,128)S(1)}, u32[]{:S(2)}, u32[]{:S(2)}) %collective-permute-start.34) | collective-permute-done | bytes 97312 | tf_op jit(solution)/shard_map/ppermute | solution.py:21
  (446 shorter events, 82.1 us)
Async XLA Ops:
  1.4 17.4 %collective-permute-start.1 = (s32[1,16,128]{2,1,0:T(8,128)S(1)}, s32[1,16,128]{2,1,0:T(8,128)S(1)}, u32[]{:S(2)}, u32[]{:S(2)}) collective-permute-start(s32[1,16,128]{2,1,0:T(8,128)S(1)} %get-tuple-element.317), channel_id=1, source_target_pairs={{4,0},{8,4},{12,8},{0,12},{5,1},{9,5},{13,9},{1,13},{6,2},{10,6},{... | collective-permute-start | bytes 24584 | tf_op jit(solution)/shard_map/ppermute | solution.py:23
  5.6 13.2 %collective-permute-start = (s32[1,16,128]{2,1,0:T(8,128)S(1)}, s32[1,16,128]{2,1,0:T(8,128)S(1)}, u32[]{:S(2)}, u32[]{:S(2)}) collective-permute-start(s32[1,16,128]{2,1,0:T(8,128)S(1)} %get-tuple-element.318), channel_id=1, source_target_pairs={{0,4},{4,8},{8,12},{12,0},{1,5},{5,9},{9,13},{13,1},{2,6},{6,10},{... | collective-permute-start | bytes 24584 | tf_op jit(solution)/shard_map/ppermute | solution.py:21
  7.3 11.9 %collective-permute-start.5 = (f32[1,16,128]{2,1,0:T(8,128)S(1)}, f32[1,16,128]{2,1,0:T(8,128)S(1)}, u32[]{:S(2)}, u32[]{:S(2)}) collective-permute-start(f32[1,16,128]{2,1,0:T(8,128)S(1)} %get-tuple-element.308), channel_id=1, source_target_pairs={{0,4},{4,8},{8,12},{12,0},{1,5},{5,9},{9,13},{13,1},{2,6},{6,10},{... | collective-permute-start | bytes 24584 | tf_op jit(solution)/shard_map/ppermute | solution.py:21
  7.4 11.8 %collective-permute-start.4 = (f32[1,16,128]{2,1,0:T(8,128)S(1)}, f32[1,16,128]{2,1,0:T(8,128)S(1)}, u32[]{:S(2)}, u32[]{:S(2)}) collective-permute-start(f32[1,16,128]{2,1,0:T(8,128)S(1)} %get-tuple-element.309), channel_id=1, source_target_pairs={{4,0},{8,4},{12,8},{0,12},{5,1},{9,5},{13,9},{1,13},{6,2},{10,6},{... | collective-permute-start | bytes 24584 | tf_op jit(solution)/shard_map/ppermute | solution.py:23
  19.2 4.8 %collective-permute-start.7 = (f32[10,1,128]{2,1,0:T(1,128)S(1)}, f32[10,1,128]{2,1,0:T(1,128)S(1)}, u32[]{:S(2)}, u32[]{:S(2)}) collective-permute-start(f32[10,1,128]{2,1,0:T(1,128)S(1)} %get-tuple-element.222), channel_id=1, source_target_pairs={{0,1},{1,2},{2,3},{3,0},{4,5},{5,6},{6,7},{7,4},{8,9},{9,10},{10,1... | collective-permute-start | bytes 15368 | tf_op jit(solution)/shard_map/ppermute | solution.py:21
  21.9 25.8 %collective-permute-start.3 = (s32[10,1,128]{2,1,0:T(1,128)S(1)}, s32[10,1,128]{2,1,0:T(1,128)S(1)}, u32[]{:S(2)}, u32[]{:S(2)}) collective-permute-start(s32[10,1,128]{2,1,0:T(1,128)S(1)} %get-tuple-element.228), channel_id=1, source_target_pairs={{1,0},{2,1},{3,2},{0,3},{5,4},{6,5},{7,6},{4,7},{9,8},{10,9},{11,1... | collective-permute-start | bytes 15368 | tf_op jit(solution)/shard_map/ppermute | solution.py:23
  22.6 25.1 %collective-permute-start.2 = (s32[10,1,128]{2,1,0:T(1,128)S(1)}, s32[10,1,128]{2,1,0:T(1,128)S(1)}, u32[]{:S(2)}, u32[]{:S(2)}) collective-permute-start(s32[10,1,128]{2,1,0:T(1,128)S(1)} %get-tuple-element.229), channel_id=1, source_target_pairs={{0,1},{1,2},{2,3},{3,0},{4,5},{5,6},{6,7},{7,4},{8,9},{9,10},{10,1... | collective-permute-start | bytes 15368 | tf_op jit(solution)/shard_map/ppermute | solution.py:21
  32.4 16.7 %collective-permute-start.8 = (f32[19,1,16,128]{3,2,1,0:T(8,128)S(1)}, f32[19,1,16,128]{3,2,1,0:T(8,128)S(1)}, u32[]{:S(2)}, u32[]{:S(2)}) collective-permute-start(f32[19,1,16,128]{3,2,1,0:T(8,128)S(1)} %get-tuple-element.131), channel_id=1, source_target_pairs={{0,4},{4,8},{8,12},{12,0},{1,5},{5,9},{9,13},{13,1},{2,6},{6,10},{... | collective-permute-start | bytes 466952 | tf_op jit(solution)/shard_map/ppermute | solution.py:21
  32.5 18.5 %collective-permute-start.9 = (f32[19,1,16,128]{3,2,1,0:T(8,128)S(1)}, f32[19,1,16,128]{3,2,1,0:T(8,128)S(1)}, u32[]{:S(2)}, u32[]{:S(2)}) collective-permute-start(f32[19,1,16,128]{3,2,1,0:T(8,128)S(1)} %get-tuple-element.132), channel_id=1, source_target_pairs={{4,0},{8,4},{12,8},{0,12},{5,1},{9,5},{13,9},{1,13},{6,2},{10,6},{... | collective-permute-start | bytes 466952 | tf_op jit(solution)/shard_map/ppermute | solution.py:23
  52.0 4.0 %collective-permute-start.11 = (f32[19,10,1,128]{3,2,1,0:T(1,128)S(1)}, f32[19,10,1,128]{3,2,1,0:T(1,128)S(1)}, u32[]{:S(2)}, u32[]{:S(2)}) collective-permute-start(f32[19,10,1,128]{3,2,1,0:T(1,128)S(1)} %get-tuple-element.124), channel_id=1, source_target_pairs={{1,0},{2,1},{3,2},{0,3},{5,4},{6,5},{7,6},{4,7},{9,8},{10,9},{11,1... | collective-permute-start | bytes 291848 | tf_op jit(solution)/shard_map/ppermute | solution.py:23
  59.0 5.7 %collective-permute-start.13 = (f32[1,16,128]{2,1,0:T(8,128)S(1)}, f32[1,16,128]{2,1,0:T(8,128)S(1)}, u32[]{:S(2)}, u32[]{:S(2)}) collective-permute-start(f32[1,16,128]{2,1,0:T(8,128)S(1)} %get-tuple-element.298), channel_id=1, source_target_pairs={{0,4},{4,8},{8,12},{12,0},{1,5},{5,9},{9,13},{13,1},{2,6},{6,10},{... | collective-permute-start | bytes 24584 | tf_op jit(solution)/shard_map/ppermute | solution.py:21
  59.0 5.7 %collective-permute-start.12 = (f32[1,16,128]{2,1,0:T(8,128)S(1)}, f32[1,16,128]{2,1,0:T(8,128)S(1)}, u32[]{:S(2)}, u32[]{:S(2)}) collective-permute-start(f32[1,16,128]{2,1,0:T(8,128)S(1)} %get-tuple-element.299), channel_id=1, source_target_pairs={{4,0},{8,4},{12,8},{0,12},{5,1},{9,5},{13,9},{1,13},{6,2},{10,6},{... | collective-permute-start | bytes 24584 | tf_op jit(solution)/shard_map/ppermute | solution.py:23
  75.7 7.9 %collective-permute-start.16 = (f32[19,1,16,128]{3,2,1,0:T(8,128)S(1)}, f32[19,1,16,128]{3,2,1,0:T(8,128)S(1)}, u32[]{:S(2)}, u32[]{:S(2)}) collective-permute-start(f32[19,1,16,128]{3,2,1,0:T(8,128)S(1)} %get-tuple-element.129), channel_id=1, source_target_pairs={{0,4},{4,8},{8,12},{12,0},{1,5},{5,9},{9,13},{13,1},{2,6},{6,10},{... | collective-permute-start | bytes 466952 | tf_op jit(solution)/shard_map/ppermute | solution.py:21
  76.6 9.1 %collective-permute-start.17 = (f32[19,1,16,128]{3,2,1,0:T(8,128)S(1)}, f32[19,1,16,128]{3,2,1,0:T(8,128)S(1)}, u32[]{:S(2)}, u32[]{:S(2)}) collective-permute-start(f32[19,1,16,128]{3,2,1,0:T(8,128)S(1)} %get-tuple-element.130), channel_id=1, source_target_pairs={{4,0},{8,4},{12,8},{0,12},{5,1},{9,5},{13,9},{1,13},{6,2},{10,6},{... | collective-permute-start | bytes 466952 | tf_op jit(solution)/shard_map/ppermute | solution.py:23
  87.3 4.0 %collective-permute-start.19 = (f32[19,10,1,128]{3,2,1,0:T(1,128)S(1)}, f32[19,10,1,128]{3,2,1,0:T(1,128)S(1)}, u32[]{:S(2)}, u32[]{:S(2)}) collective-permute-start(f32[19,10,1,128]{3,2,1,0:T(1,128)S(1)} %get-tuple-element.122), channel_id=1, source_target_pairs={{1,0},{2,1},{3,2},{0,3},{5,4},{6,5},{7,6},{4,7},{9,8},{10,9},{11,1... | collective-permute-start | bytes 291848 | tf_op jit(solution)/shard_map/ppermute | solution.py:23
  94.3 4.9 %collective-permute-start.21 = (f32[1,16,128]{2,1,0:T(8,128)S(1)}, f32[1,16,128]{2,1,0:T(8,128)S(1)}, u32[]{:S(2)}, u32[]{:S(2)}) collective-permute-start(f32[1,16,128]{2,1,0:T(8,128)S(1)} %get-tuple-element.288), channel_id=1, source_target_pairs={{0,4},{4,8},{8,12},{12,0},{1,5},{5,9},{9,13},{13,1},{2,6},{6,10},{... | collective-permute-start | bytes 24584 | tf_op jit(solution)/shard_map/ppermute | solution.py:21
  95.4 3.8 %collective-permute-start.20 = (f32[1,16,128]{2,1,0:T(8,128)S(1)}, f32[1,16,128]{2,1,0:T(8,128)S(1)}, u32[]{:S(2)}, u32[]{:S(2)}) collective-permute-start(f32[1,16,128]{2,1,0:T(8,128)S(1)} %get-tuple-element.289), channel_id=1, source_target_pairs={{4,0},{8,4},{12,8},{0,12},{5,1},{9,5},{13,9},{1,13},{6,2},{10,6},{... | collective-permute-start | bytes 24584 | tf_op jit(solution)/shard_map/ppermute | solution.py:23
  111.0 7.9 %collective-permute-start.24 = (f32[19,1,16,128]{3,2,1,0:T(8,128)S(1)}, f32[19,1,16,128]{3,2,1,0:T(8,128)S(1)}, u32[]{:S(2)}, u32[]{:S(2)}) collective-permute-start(f32[19,1,16,128]{3,2,1,0:T(8,128)S(1)} %get-tuple-element.127), channel_id=1, source_target_pairs={{0,4},{4,8},{8,12},{12,0},{1,5},{5,9},{9,13},{13,1},{2,6},{6,10},{... | collective-permute-start | bytes 466952 | tf_op jit(solution)/shard_map/ppermute | solution.py:21
  111.1 8.7 %collective-permute-start.25 = (f32[19,1,16,128]{3,2,1,0:T(8,128)S(1)}, f32[19,1,16,128]{3,2,1,0:T(8,128)S(1)}, u32[]{:S(2)}, u32[]{:S(2)}) collective-permute-start(f32[19,1,16,128]{3,2,1,0:T(8,128)S(1)} %get-tuple-element.128), channel_id=1, source_target_pairs={{4,0},{8,4},{12,8},{0,12},{5,1},{9,5},{13,9},{1,13},{6,2},{10,6},{... | collective-permute-start | bytes 466952 | tf_op jit(solution)/shard_map/ppermute | solution.py:23
  121.3 4.0 %collective-permute-start.27 = (f32[19,10,1,128]{3,2,1,0:T(1,128)S(1)}, f32[19,10,1,128]{3,2,1,0:T(1,128)S(1)}, u32[]{:S(2)}, u32[]{:S(2)}) collective-permute-start(f32[19,10,1,128]{3,2,1,0:T(1,128)S(1)} %get-tuple-element.120), channel_id=1, source_target_pairs={{1,0},{2,1},{3,2},{0,3},{5,4},{6,5},{7,6},{4,7},{9,8},{10,9},{11,1... | collective-permute-start | bytes 291848 | tf_op jit(solution)/shard_map/ppermute | solution.py:23
  128.3 5.2 %collective-permute-start.29 = (f32[1,16,128]{2,1,0:T(8,128)S(1)}, f32[1,16,128]{2,1,0:T(8,128)S(1)}, u32[]{:S(2)}, u32[]{:S(2)}) collective-permute-start(f32[1,16,128]{2,1,0:T(8,128)S(1)} %get-tuple-element.278), channel_id=1, source_target_pairs={{0,4},{4,8},{8,12},{12,0},{1,5},{5,9},{9,13},{13,1},{2,6},{6,10},{... | collective-permute-start | bytes 24584 | tf_op jit(solution)/shard_map/ppermute | solution.py:21
  146.3 7.6 %collective-permute-start.32 = (f32[19,1,16,128]{3,2,1,0:T(8,128)S(1)}, f32[19,1,16,128]{3,2,1,0:T(8,128)S(1)}, u32[]{:S(2)}, u32[]{:S(2)}) collective-permute-start(f32[19,1,16,128]{3,2,1,0:T(8,128)S(1)} %get-tuple-element.125), channel_id=1, source_target_pairs={{0,4},{4,8},{8,12},{12,0},{1,5},{5,9},{9,13},{13,1},{2,6},{6,10},{... | collective-permute-start | bytes 466952 | tf_op jit(solution)/shard_map/ppermute | solution.py:21
  147.2 8.2 %collective-permute-start.33 = (f32[19,1,16,128]{3,2,1,0:T(8,128)S(1)}, f32[19,1,16,128]{3,2,1,0:T(8,128)S(1)}, u32[]{:S(2)}, u32[]{:S(2)}) collective-permute-start(f32[19,1,16,128]{3,2,1,0:T(8,128)S(1)} %get-tuple-element.126), channel_id=1, source_target_pairs={{4,0},{8,4},{12,8},{0,12},{5,1},{9,5},{13,9},{1,13},{6,2},{10,6},{... | collective-permute-start | bytes 466952 | tf_op jit(solution)/shard_map/ppermute | solution.py:23
  156.8 4.0 %collective-permute-start.35 = (f32[19,10,1,128]{3,2,1,0:T(1,128)S(1)}, f32[19,10,1,128]{3,2,1,0:T(1,128)S(1)}, u32[]{:S(2)}, u32[]{:S(2)}) collective-permute-start(f32[19,10,1,128]{3,2,1,0:T(1,128)S(1)} %get-tuple-element.118), channel_id=1, source_target_pairs={{1,0},{2,1},{3,2},{0,3},{5,4},{6,5},{7,6},{4,7},{9,8},{10,9},{11,1... | collective-permute-start | bytes 291848 | tf_op jit(solution)/shard_map/ppermute | solution.py:23
  (20 other events, 96.0 us)
where the time goes:
time: 168 us; the launch traced here: 165 us
  starting transfers between devices  56.8 us (34%)
  waiting for transfers between devices  43.4 us (26%)
  matrix products  26.7 us (16%)
  other arithmetic  26.2 us (16%)
  local copies, waits for them, and re-layouts  8.24 us (5%)
  between operations  3.52 us (2%)
    ppermute x18, starting transfers between devices, extended(): lax.ppermute(head, axis, [((i + 1) % count, i) for i in range(count)])  40 us
    ppermute x18, waiting for transfers between devices, extended(): lax.ppermute(head, axis, [((i + 1) % count, i) for i in range(count)])  23.5 us
    ppermute x18, waiting for transfers between devices, extended(): lax.ppermute(tail, axis, [(i, (i + 1) % count) for i in range(count)])  20 us
    ppermute x18, starting transfers between devices, extended(): lax.ppermute(tail, axis, [(i, (i + 1) % count) for i in range(count)])  16.8 us
    dot_general x4, matrix products, collision(): jnp.dot(collide, excess.reshape(shape[0], -1), precision=lax.Precision.HI...  7.89 us
    dot_general x4, matrix products, collision(): jnp.einsum('kc,kxyz->cxyz', lattice_vel, populations, precision=lax.Preci...  6.46 us
    dot_general x4, matrix products, collision(): jnp.einsum('kc,cxyz->kxyz', lattice_vel, speed, precision=lax.Precision.H...  5.9 us
    dot_general x4, matrix products, collision(): jnp.einsum('kc,cxyz->kxyz', lattice_vel, force, precision=lax.Precision.H...  5.9 us
  transfers between devices with their start and end apart: 36, of which 22 were waited for; matrix products, arithmetic and copies ran while one was open for 15% of the time, Pallas kernels for 0%

commit v1 on v0

v1 whole, which is shorter than its diff:
```python
import functools

import jax
import jax.numpy as jnp
from jax import lax
from jax.experimental import pallas as pl
from jax.experimental.pallas import tpu as pltpu
from jax.sharding import PartitionSpec as P

WET_CLASSES = 4
STEPS = 4
COUPLING = 2.5
PAD = 8
VEL = [
    (0, 0, 0),
    (1, 0, 0),
    (-1, 0, 0),
    (0, 1, 0),
    (0, -1, 0),
    (0, 0, 1),
    (0, 0, -1),
    (1, 1, 0),
    (-1, -1, 0),
    (1, -1, 0),
    (-1, 1, 0),
    (1, 0, 1),
    (-1, 0, -1),
    (1, 0, -1),
    (-1, 0, 1),
    (0, 1, 1),
    (0, -1, -1),
    (0, 1, -1),
    (0, -1, 1),
]
INDEX = {v: k for k, v in enumerate(VEL)}
OPP = [INDEX[(-a, -b, -c)] for a, b, c in VEL]
ORDER = (
    [k for k in range(19) if VEL[k][0] == 1]
    + [k for k in range(19) if VEL[k][0] == -1]
    + [k for k in range(19) if VEL[k][0] == 0]
)
PLACE = [ORDER.index(k) for k in range(19)]
CROSS = [[k for k in range(19) if VEL[k][1] == s] for s in (-1, 1)]
CORNERS = [(1, 1), (1, -1), (-1, 1), (-1, -1)]
SENDS = [(1, 0), (-1, 0), (0, 1), (0, -1)] + CORNERS


def roll_z(value, step):
    if step == 0:
        return value
    return pltpu.roll(value, step % value.shape[-1], axis=value.ndim - 1)


def to_moments(f):
    g = lambda *v: f[INDEX[v]]
    m = {}

    def plane(pp, mm, pm, mp):
        a, b, c, d = pp + mm, pm + mp, pp - mm, pm - mp
        return a + b, a - b, c + d, c - d

    m["xxyy"], m["xy"], m["xyy"], m["yxx"] = plane(
        g(1, 1, 0), g(-1, -1, 0), g(1, -1, 0), g(-1, 1, 0)
    )
    m["xxzz"], m["xz"], m["xzz"], m["zxx"] = plane(
        g(1, 0, 1), g(-1, 0, -1), g(1, 0, -1), g(-1, 0, 1)
    )
    m["yyzz"], m["yz"], m["yzz"], m["zyy"] = plane(
        g(0, 1, 1), g(0, -1, -1), g(0, 1, -1), g(0, -1, 1)
    )
    sx, dx = f[1] + f[2], f[1] - f[2]
    sy, dy = f[3] + f[4], f[3] - f[4]
    sz, dz = f[5] + f[6], f[5] - f[6]
    m["xx"] = sx + (m["xxyy"] + m["xxzz"])
    m["yy"] = sy + (m["xxyy"] + m["yyzz"])
    m["zz"] = sz + (m["xxzz"] + m["yyzz"])
    m["x"] = dx + (m["xyy"] + m["xzz"])
    m["y"] = dy + (m["yxx"] + m["yzz"])
    m["z"] = dz + (m["zxx"] + m["zyy"])
    m["1"] = ((f[0] + sx) + (sy + sz)) + ((m["xxyy"] + m["xxzz"]) + m["yyzz"])
    return m


def from_moments(m):
    f = [None] * 19

    def plane(even, cross, first, second, v):
        a, b = 0.25 * (even + cross), 0.25 * (even - cross)
        c, d = 0.25 * (first + second), 0.25 * (first - second)
        values = (a + c, a - c, b + d, b - d)
        for velocity, value in zip(v, values):
            f[INDEX[velocity]] = value

    plane(m["xxyy"], m["xy"], m["xyy"], m["yxx"], [(1, 1, 0), (-1, -1, 0), (1, -1, 0), (-1, 1, 0)])
    plane(m["xxzz"], m["xz"], m["xzz"], m["zxx"], [(1, 0, 1), (-1, 0, -1), (1, 0, -1), (-1, 0, 1)])
    plane(m["yyzz"], m["yz"], m["yzz"], m["zyy"], [(0, 1, 1), (0, -1, -1), (0, 1, -1), (0, -1, 1)])
    sx = m["xx"] - (m["xxyy"] + m["xxzz"])
    sy = m["yy"] - (m["xxyy"] + m["yyzz"])
    sz = m["zz"] - (m["xxzz"] + m["yyzz"])
    dx = m["x"] - (m["xyy"] + m["xzz"])
    dy = m["y"] - (m["yxx"] + m["yzz"])
    dz = m["z"] - (m["zxx"] + m["zyy"])
    f[1], f[2] = 0.5 * (sx + dx), 0.5 * (sx - dx)
    f[3], f[4] = 0.5 * (sy + dy), 0.5 * (sy - dy)
    f[5], f[6] = 0.5 * (sz + dz), 0.5 * (sz - dz)
    f[0] = (m["1"] - (sx + sy)) - (sz + ((m["xxyy"] + m["xxzz"]) + m["yyzz"]))
    return f


NAMES = [
    "1", "x", "y", "z", "xy", "xz", "yz", "xx", "yy", "zz",
    "xyy", "xzz", "yxx", "yzz", "zxx", "zyy", "xxyy", "xxzz", "yyzz",
]


def collide(f, fluid, near, rates):
    third = 1.0 / 3.0
    m = to_moments(f)
    here = near(0, 0)
    xp, xm, yp, ym = near(1, 0), near(-1, 0), near(0, 1), near(0, -1)
    dx, dy = xp - xm, yp - ym
    ring = (2.0 * here + (xp + xm)) + (yp + ym)
    pp, pm, mp, mm = near(1, 1), near(1, -1), near(-1, 1), near(-1, -1)
    a, b = pp - mm, pm - mp
    scale = (COUPLING / 36.0) * here
    fx = scale * ((2.0 * dx + (a + b)) + (roll_z(dx, 1) + roll_z(dx, -1)))
    fy = scale * ((2.0 * dy + (a - b)) + (roll_z(dy, 1) + roll_z(dy, -1)))
    fz = scale * (roll_z(ring, -1) - roll_z(ring, 1))
    rho = jnp.where(fluid, m["1"], 1.0)
    inv = 1.0 / rho
    ux, uy, uz = ((m[n] + 0.5 * v) * inv for n, v in (("x", fx), ("y", fy), ("z", fz)))
    jx, jy, jz = rho * ux, rho * uy, rho * uz
    qx, qy, qz = jx * ux, jy * uy, jz * uz
    wx, wy, wz = ux * fx, uy * fy, uz * fz
    rho3, rho9 = rho * third, rho * (1.0 / 9.0)
    hx, hy, hz = (0.5 * q for q in (qx, qy, qz))
    hsum = rho9 - third * (hx + hy + hz)
    wsum = third * (wx + wy + wz)
    equil = {
        "1": rho, "x": jx, "y": jy, "z": jz,
        "xy": jx * uy, "xz": jx * uz, "yz": jy * uz,
        "xx": rho3 + qx, "yy": rho3 + qy, "zz": rho3 + qz,
        "xyy": jx * third, "yxx": jy * third, "zxx": jz * third,
        "xxyy": hsum + (hx + hy), "xxzz": hsum + (hx + hz), "yyzz": hsum + (hy + hz),
    }
    source = {
        "1": None, "x": fx, "y": fy, "z": fz,
        "xy": fx * uy + fy * ux, "xz": fx * uz + fz * ux, "yz": fy * uz + fz * uy,
        "xx": 2.0 * wx, "yy": 2.0 * wy, "zz": 2.0 * wz,
        "xyy": fx * third, "yxx": fy * third, "zxx": fz * third,
        "xxyy": (wx + wy) - wsum, "xxzz": (wx + wz) - wsum, "yyzz": (wy + wz) - wsum,
    }
    for table in (equil, source):
        table["xzz"], table["yzz"], table["zyy"] = table["xyy"], table["yxx"], table["zxx"]
    after = {}
    for row, name in enumerate(NAMES):
        rate = rates[row]
        if source[name] is None:
            after[name] = m[name] + rate * (equil[name] - m[name])
        else:
            after[name] = (m[name] + source[name]) + rate * (
                (equil[name] - m[name]) - 0.5 * source[name]
            )
    return from_moments(after), (ux, uy, uz)


def kernel(
    counts, pop_ref, mask_ref, wet_ref, wall_ref, rate_ref, out_ref, vel_ref,
    pot, f_buf, bits, post, pot_ysend, pot_yrecv, pot_crecv, ysend, yrecv, crecv,
    send_sem, recv_sem,
):
    nx, ny = mask_ref.shape[0], mask_ref.shape[1]
    halves = ny // 8
    top = PAD + ny
    gx, gy = lax.axis_index("gx"), lax.axis_index("gy")

    def neighbour(d):
        return {
            "gx": lax.rem(gx + d[0] + counts[0], counts[0]),
            "gy": lax.rem(gy + d[1] + counts[1], counts[1]),
        }

    barrier = pltpu.get_barrier_semaphore()
    for d in SENDS:
        pl.semaphore_signal(
            barrier, inc=1, device_id=neighbour(d), device_id_type=pl.DeviceIdType.MESH
        )

    def copies(kind, slot, pairs):
        made = []
        for i, d in enumerate(SENDS):
            made.append(
                pltpu.make_async_remote_copy(
                    src_ref=pairs[d][0],
                    dst_ref=pairs[d][1],
                    send_sem=send_sem.at[kind, slot, i],
                    recv_sem=recv_sem.at[kind, slot, i],
                    device_id=neighbour(d),
                    device_id_type=pl.DeviceIdType.MESH,
                )
            )
        return made

    rows = pl.ds(PAD, ny)

    def pot_copies(slot, wide):
        parts = pl.ds(0, 2 if wide else 1)
        pairs = {
            (1, 0): (pot.at[slot, parts, nx, rows], pot.at[slot, parts, 0, rows]),
            (-1, 0): (pot.at[slot, parts, 1, rows], pot.at[slot, parts, nx + 1, rows]),
        }
        for side, s in enumerate((-1, 1)):
            tile = pot_ysend.at[slot, side, parts]
            pairs[(0, s)] = (tile, pot_yrecv.at[slot, side, parts])
            for c, d in enumerate(CORNERS):
                if d[1] == s:
                    pairs[d] = (tile, pot_crecv.at[slot, c, parts])
        return copies(0, slot, pairs)

    def post_copies(slot):
        ahead, back = pl.ds(0, 5), pl.ds(5, 5)
        pairs = {
            (1, 0): (post.at[slot, ahead, nx, rows], post.at[slot, ahead, 0, rows]),
            (-1, 0): (post.at[slot, back, 1, rows], post.at[slot, back, nx + 1, rows]),
        }
        for side, s in enumerate((-1, 1)):
            pairs[(0, s)] = (ysend.at[slot, side], yrecv.at[slot, side])
            for c, d in enumerate(CORNERS):
                if d[1] == s:
                    j = CROSS[side].index(INDEX[(d[0], d[1], 0)])
                    pairs[d] = (ysend.at[slot, side, j], crecv.at[slot, c])
        return copies(1, slot, pairs)

    def pot_unpack(slot, wide):
        for part in range(2 if wide else 1):
            for side, ghost in enumerate((top, PAD - 1)):
                for x in range(nx):
                    pot[slot, part, x + 1, ghost : ghost + 1, :] = pot_yrecv[
                        slot, side, part, x : x + 1, :
                    ]
            for c, (dx, dy) in enumerate(CORNERS):
                row = nx - 1 if dx == 1 else 0
                ghost = PAD - 1 if dy == 1 else top
                pot[slot, part, 0 if dx == 1 else nx + 1, ghost : ghost + 1, :] = pot_crecv[
                    slot, c, part, row : row + 1, :
                ]

    def post_unpack(slot):
        for side, ghost in enumerate((top, PAD - 1)):
            for j, k in enumerate(CROSS[side]):
                for x in range(nx):
                    post[slot, PLACE[k], x + 1, ghost : ghost + 1, :] = yrecv[
                        slot, side, j, x : x + 1, :
                    ]
        for c, (dx, dy) in enumerate(CORNERS):
            row = nx - 1 if dx == 1 else 0
            ghost = PAD - 1 if dy == 1 else top
            k = INDEX[(dx, dy, 0)]
            post[slot, PLACE[k], 0 if dx == 1 else nx + 1, ghost : ghost + 1, :] = crecv[
                slot, c, row : row + 1, :
            ]

    def each_block(body):
        def plane(x, carry):
            for h in range(halves):
                body(x, h)
            return carry

        lax.fori_loop(0, nx, plane, 0)

    def put_edges(target, x, h, value):
        if h == 0:
            target(0)[pl.ds(x, 1), :] = value[0:1]
        if h == halves - 1:
            target(1)[pl.ds(x, 1), :] = value[7:8]

    def potential(slot, x, h, f, wide):
        block = pl.ds(8 * h, 8)
        fluid = mask_ref[x, block, :] == 1
        density = f[0]
        for k in range(1, 19):
            density = density + f[k]
        wet = wet_ref[x, block, :]
        wall = jnp.zeros_like(density)
        for c in range(WET_CLASSES):
            wall = wall + jnp.where(wet == c, wall_ref[c], 0.0)
        safe = jnp.where(fluid, density, 1.0)
        value = jnp.where(fluid, 1.0 - jnp.exp(-safe), wall)
        pot[slot, 0, x + 1, pl.ds(PAD + 8 * h, 8), :] = value
        put_edges(lambda side: pot_ysend.at[slot, side, 0], x, h, value)
        if wide:
            flag = jnp.where(fluid, 1.0, 0.0)
            pot[slot, 1, x + 1, pl.ds(PAD + 8 * h, 8), :] = flag
            put_edges(lambda side: pot_ysend.at[slot, side, 1], x, h, flag)

    def streamed(slot, x, h):
        flags = bits[x, pl.ds(8 * h, 8), :]
        f = []
        for k, (ex, ey, ez) in enumerate(VEL):
            if k == 0:
                f.append(post[slot, PLACE[0], x + 1, pl.ds(PAD + 8 * h, 8), :])
                continue
            passed = roll_z(post[slot, PLACE[k], x + 1 - ex, pl.ds(PAD + 8 * h - ey, 8), :], ez)
            bounced = post[slot, PLACE[OPP[k]], x + 1, pl.ds(PAD + 8 * h, 8), :]
            f.append(jnp.where((flags & (1 << k)) != 0, passed, bounced))
        return f

    def first(x, h):
        potential(0, x, h, [pop_ref[k, x, pl.ds(8 * h, 8), :] for k in range(19)], True)

    def inflow(x, h):
        flags = jnp.zeros((8, mask_ref.shape[2]), jnp.int32)
        for k, (ex, ey, ez) in enumerate(VEL):
            if k > 0:
                flag = roll_z(pot[0, 1, x + 1 - ex, pl.ds(PAD + 8 * h - ey, 8), :], ez)
                flags = flags | jnp.where(flag == 1.0, 1 << k, 0)
        bits[x, pl.ds(8 * h, 8), :] = flags

    def collision(step, x, h):
        slot = step % 2
        block = pl.ds(8 * h, 8)
        source = pop_ref if step == 0 else f_buf
        fluid = mask_ref[x, block, :] == 1
        near = lambda dx, dy: pot[slot, 0, x + 1 + dx, pl.ds(PAD + 8 * h + dy, 8), :]
        rates = [rate_ref[r] for r in range(19)]
        f, speed = collide([source[k, x, block, :] for k in range(19)], fluid, near, rates)
        for k in range(19):
            post[slot, PLACE[k], x + 1, pl.ds(PAD + 8 * h, 8), :] = f[k]
            for side in range(2):
                if k in CROSS[side] and h == (0, halves - 1)[side]:
                    row = (0, 7)[side]
                    ysend[slot, side, CROSS[side].index(k), pl.ds(x, 1), :] = f[k][row : row + 1]
        if step == STEPS - 1:
            for c in range(3):
                vel_ref[c, x, block, :] = jnp.where(fluid, speed[c], 0.0)

    def stream(step, x, h):
        f = streamed((step - 1) % 2, x, h)
        for k in range(19):
            f_buf[k, x, pl.ds(8 * h, 8), :] = f[k]
        potential(step % 2, x, h, f, False)

    def last(x, h):
        f = streamed((STEPS - 1) % 2, x, h)
        block = pl.ds(8 * h, 8)
        fluid = mask_ref[x, block, :] == 1
        for k in range(19):
            out_ref[k, x, block, :] = jnp.where(fluid, f[k], 0.0)

    each_block(first)
    pl.semaphore_wait(barrier, len(SENDS))
    for step in range(STEPS):
        slot = step % 2
        if step > 0:
            each_block(functools.partial(stream, step))
        moving = pot_copies(slot, step == 0)
        for copy in moving:
            copy.start()
        for copy in moving:
            copy.wait()
        pot_unpack(slot, step == 0)
        if step == 0:
            each_block(inflow)
        each_block(functools.partial(collision, step))
        moving = post_copies(slot)
        for copy in moving:
            copy.start()
        for copy in moving:
            copy.wait()
        post_unpack(slot)
    each_block(last)


def per_device(counts, populations, fluid_mask, wet_class, wall_potential, relax_rates):
    nx, ny, nz = fluid_mask.shape
    vmem = pl.BlockSpec(memory_space=pltpu.VMEM)
    smem = pl.BlockSpec(memory_space=pltpu.SMEM)
    f32 = jnp.float32
    padded = (nx + 2, ny + 2 * PAD, nz)
    return pl.pallas_call(
        functools.partial(kernel, counts),
        out_shape=(
            jax.ShapeDtypeStruct((19, nx, ny, nz), f32),
            jax.ShapeDtypeStruct((3, nx, ny, nz), f32),
        ),
        in_specs=[vmem, vmem, vmem, smem, smem],
        out_specs=(vmem, vmem),
        scratch_shapes=[
            pltpu.VMEM((2, 2) + padded, f32),
            pltpu.VMEM((19, nx, ny, nz), f32),
            pltpu.VMEM((nx, ny, nz), jnp.int32),
            pltpu.VMEM((2, 19) + padded, f32),
            pltpu.VMEM((2, 2, 2, nx, nz), f32),
            pltpu.VMEM((2, 2, 2, nx, nz), f32),
            pltpu.VMEM((2, 4, 2, nx, nz), f32),
            pltpu.VMEM((2, 2, 5, nx, nz), f32),
            pltpu.VMEM((2, 2, 5, nx, nz), f32),
            pltpu.VMEM((2, 4, nx, nz), f32),
            pltpu.SemaphoreType.DMA((2, 2, len(SENDS))),
            pltpu.SemaphoreType.DMA((2, 2, len(SENDS))),
        ],
        compiler_params=pltpu.CompilerParams(
            collective_id=0, has_side_effects=True, vmem_limit_bytes=48 * 1024 * 1024
        ),
    )(populations, fluid_mask, wet_class, wall_potential, relax_rates)


def solution(mesh):
    counts = (mesh.shape["gx"], mesh.shape["gy"])
    return jax.shard_map(
        functools.partial(per_device, counts),
        mesh=mesh,
        in_specs=(
            P(None, ("groups", "gx"), "gy", None),
            P(("groups", "gx"), "gy", None),
            P(("groups", "gx"), "gy", None),
            P("groups"),
            P(),
        ),
        out_specs=(P(None, ("groups", "gx"), "gy", None), P(None, ("groups", "gx"), "gy", None)),
        check_vma=False,
    )
```

time: 168 us -> 58.9 us (0.35); the launches traced: 165 us -> 58.6 us
  starting transfers between devices: 56.8 us -> 0 us
  Pallas kernels: 0 us -> 52 us
  waiting for transfers between devices: 43.4 us -> 0 us
  matrix products: 26.7 us -> 0 us
  other arithmetic: 26.2 us -> 0 us
  between operations: 3.52 us -> 0.65 us
  local copies, waits for them, and re-layouts: 8.24 us -> 5.99 us
    ppermute x36 -> x0, starting transfers between devices: 56.8 us -> none  [the longest x18 40 us: extended(): lax.ppermute(head, axis, [((i + 1) % count, i) for i in range(count)])]
    pallas_call x0 -> x1, Pallas kernels: none -> 52 us  [per_device(): pl.pallas_call(functools.partial(kernel, counts), out_shape=(jax.ShapeDty...]
    ppermute x36 -> x0, waiting for transfers between devices: 43.4 us -> none  [the longest x18 23.5 us: extended(): lax.ppermute(head, axis, [((i + 1) % count, i) for i in range(count)])]
    dot_general x17 -> x0, matrix products: 26.4 us -> none  [the longest x4 7.89 us: collision(): jnp.dot(collide, excess.reshape(shape[0], -1), precision=lax.Precision.HI...]
    another operation x18 -> x0, other arithmetic: 6.8 us -> none  [the longest x3 3.11 us: collide_matrix(): factor = jnp.linalg.cholesky(gram)]
    slice x105 -> x0, local copies, waits for them, and re-layouts: 5.81 us -> none  [the longest x95 4.94 us: offset_view(): return jnp.roll(window, -step_z, axis=-1)]
    unnamed x129 -> x12, local copies, waits for them, and re-layouts: 1.11 us -> 5.99 us
    unnamed x53 -> x0, other arithmetic: 4.07 us -> none
  transfers between devices with their start and end apart: 36 -> 0, of which waited for: 22 -> 0; matrix products, arithmetic and copies ran while one was open for 15% -> 0% of each run, Pallas kernels for 0% -> 0%
where the time goes in v1:
time: 58.9 us; the launch traced here: 58.6 us
  Pallas kernels  52 us (88%)
  local copies, waits for them, and re-layouts  5.99 us (10%)
  between operations  0.65 us (1%)
    pallas_call x1, Pallas kernels, per_device(): pl.pallas_call(functools.partial(kernel, counts), out_shape=(jax.ShapeDty...  52 us
    unnamed x12, local copies, waits for them, and re-layouts  5.99 us

profile of v1, /device:TPU:1, one launch (start us, length us, event | category | flops | bytes accessed | tf_op | source)
XLA Modules:
  0.0 58.6 jit_solution(5860067300567584423)
XLA Ops:
  0.6 0.0 copy-start
  0.6 1.3 %copy-done = f32[19,8,16,128]{3,2,1,0:T(8,128)S(1)} copy-done((f32[19,8,16,128]{3,2,1,0:T(8,128)S(1)}, f32[19,8,16,128]{3,2,1,0:T(8,128)}, u32[]{:S(2)}) %copy-start) | copy-done | bytes 1245208
  1.9 0.0 copy-start.1
  1.9 0.8 %copy-done.1 = s32[8,16,128]{2,1,0:T(8,128)S(1)} copy-done((s32[8,16,128]{2,1,0:T(8,128)S(1)}, s32[8,16,128]{2,1,0:T(8,128)}, u32[]{:S(2)}) %copy-start.1) | copy-done | bytes 65560
  2.8 0.0 copy-start.2
  2.8 0.8 %copy-done.2 = s32[8,16,128]{2,1,0:T(8,128)S(1)} copy-done((s32[8,16,128]{2,1,0:T(8,128)S(1)}, s32[8,16,128]{2,1,0:T(8,128)}, u32[]{:S(2)}) %copy-start.2) | copy-done | bytes 65560
  3.6 0.0 copy-start.3
  3.6 0.7 %copy-done.3 = f32[4]{0:T(128)S(1)} copy-done((f32[4]{0:T(128)S(1)}, f32[4]{0:T(128)}, u32[]{:S(2)}) %copy-start.3) | copy-done | bytes 40
  4.3 0.0 copy-start.4
  4.3 0.7 %copy-done.4 = f32[19]{0:T(128)S(1)} copy-done((f32[19]{0:T(128)S(1)}, f32[19]{0:T(128)}, u32[]{:S(2)}) %copy-start.4) | copy-done | bytes 100
  4.9 52.0 %shard_map.68 = (f32[19,8,16,128]{3,2,1,0:T(8,128)S(1)}, f32[3,8,16,128]{3,2,1,0:T(8,128)S(1)}) custom-call(f32[19,8,16,128]{3,2,1,0:T(8,128)S(1)} %copy-done, s32[8,16,128]{2,1,0:T(8,128)S(1)} %copy-done.1, s32[8,16,128]{2,1,0:T(8,128)S(1)} %copy-done.2, f32[4]{0:T(128)S(1)} %copy-done.3, f32[19]{0:T(128)S(1)} %copy-done.4), custom_call_target="tpu_custom_call" | custom-call | tf_op jit(solution)/shard_map/pallas_call | solution.py:380
  56.9 1.0 %copy.9 = f32[19,8,16,128]{3,2,1,0:T(8,128)} copy(f32[19,8,16,128]{3,2,1,0:T(8,128)S(1)} %get-tuple-element.4) | data formatting | bytes 2490368
  57.9 0.7 %copy.10 = f32[3,8,16,128]{3,2,1,0:T(8,128)} copy(f32[3,8,16,128]{3,2,1,0:T(8,128)S(1)} %get-tuple-element.5) | data formatting | bytes 393216
Async XLA Ops:
  0.6 1.3 %copy-start = (f32[19,8,16,128]{3,2,1,0:T(8,128)S(1)}, f32[19,8,16,128]{3,2,1,0:T(8,128)}, u32[]{:S(2)}) copy-start(f32[19,8,16,128]{3,2,1,0:T(8,128)} %pop_ref.1) | copy-start | bytes 3735556
  1.9 0.8 %copy-start.1 = (s32[8,16,128]{2,1,0:T(8,128)S(1)}, s32[8,16,128]{2,1,0:T(8,128)}, u32[]{:S(2)}) copy-start(s32[8,16,128]{2,1,0:T(8,128)} %mask_ref.1) | copy-start | bytes 196612
  2.8 0.8 %copy-start.2 = (s32[8,16,128]{2,1,0:T(8,128)S(1)}, s32[8,16,128]{2,1,0:T(8,128)}, u32[]{:S(2)}) copy-start(s32[8,16,128]{2,1,0:T(8,128)} %wet_ref.1) | copy-start | bytes 196612
  3.6 0.7 %copy-start.3 = (f32[4]{0:T(128)S(1)}, f32[4]{0:T(128)}, u32[]{:S(2)}) copy-start(f32[4]{0:T(128)} %wall_ref.1) | copy-start | bytes 52
  4.3 0.7 %copy-start.4 = (f32[19]{0:T(128)S(1)}, f32[19]{0:T(128)}, u32[]{:S(2)}) copy-start(f32[19]{0:T(128)} %rate_ref.1) | copy-start | bytes 232

commit v2 on v1

v2 whole, which is shorter than its diff:
```python
import functools

import jax
import jax.numpy as jnp
from jax import lax
from jax.experimental import pallas as pl
from jax.experimental.pallas import tpu as pltpu
from jax.sharding import PartitionSpec as P

WET_CLASSES = 4
STEPS = 4
COUPLING = 2.5
PAD = 8
VEL = [
    (0, 0, 0),
    (1, 0, 0),
    (-1, 0, 0),
    (0, 1, 0),
    (0, -1, 0),
    (0, 0, 1),
    (0, 0, -1),
    (1, 1, 0),
    (-1, -1, 0),
    (1, -1, 0),
    (-1, 1, 0),
    (1, 0, 1),
    (-1, 0, -1),
    (1, 0, -1),
    (-1, 0, 1),
    (0, 1, 1),
    (0, -1, -1),
    (0, 1, -1),
    (0, -1, 1),
]
INDEX = {v: k for k, v in enumerate(VEL)}
OPP = [INDEX[(-a, -b, -c)] for a, b, c in VEL]
ORDER = (
    [k for k in range(19) if VEL[k][0] == 1]
    + [k for k in range(19) if VEL[k][0] == -1]
    + [k for k in range(19) if VEL[k][0] == 0]
)
PLACE = [ORDER.index(k) for k in range(19)]
CROSS = [[k for k in range(19) if VEL[k][1] == s] for s in (-1, 1)]
CORNERS = [(1, 1), (1, -1), (-1, 1), (-1, -1)]
SENDS = [(1, 0), (-1, 0), (0, 1), (0, -1)] + CORNERS


def roll_z(value, step):
    if step == 0:
        return value
    return pltpu.roll(value, step % value.shape[-1], axis=value.ndim - 1)


def to_moments(f):
    g = lambda *v: f[INDEX[v]]
    m = {}

    def plane(pp, mm, pm, mp):
        a, b, c, d = pp + mm, pm + mp, pp - mm, pm - mp
        return a + b, a - b, c + d, c - d

    m["xxyy"], m["xy"], m["xyy"], m["yxx"] = plane(
        g(1, 1, 0), g(-1, -1, 0), g(1, -1, 0), g(-1, 1, 0)
    )
    m["xxzz"], m["xz"], m["xzz"], m["zxx"] = plane(
        g(1, 0, 1), g(-1, 0, -1), g(1, 0, -1), g(-1, 0, 1)
    )
    m["yyzz"], m["yz"], m["yzz"], m["zyy"] = plane(
        g(0, 1, 1), g(0, -1, -1), g(0, 1, -1), g(0, -1, 1)
    )
    sx, dx = f[1] + f[2], f[1] - f[2]
    sy, dy = f[3] + f[4], f[3] - f[4]
    sz, dz = f[5] + f[6], f[5] - f[6]
    m["xx"] = sx + (m["xxyy"] + m["xxzz"])
    m["yy"] = sy + (m["xxyy"] + m["yyzz"])
    m["zz"] = sz + (m["xxzz"] + m["yyzz"])
    m["x"] = dx + (m["xyy"] + m["xzz"])
    m["y"] = dy + (m["yxx"] + m["yzz"])
    m["z"] = dz + (m["zxx"] + m["zyy"])
    m["1"] = ((f[0] + sx) + (sy + sz)) + ((m["xxyy"] + m["xxzz"]) + m["yyzz"])
    return m


def from_moments(m):
    f = [None] * 19

    def plane(even, cross, first, second, v):
        a, b = 0.25 * (even + cross), 0.25 * (even - cross)
        c, d = 0.25 * (first + second), 0.25 * (first - second)
        values = (a + c, a - c, b + d, b - d)
        for velocity, value in zip(v, values):
            f[INDEX[velocity]] = value

    plane(m["xxyy"], m["xy"], m["xyy"], m["yxx"], [(1, 1, 0), (-1, -1, 0), (1, -1, 0), (-1, 1, 0)])
    plane(m["xxzz"], m["xz"], m["xzz"], m["zxx"], [(1, 0, 1), (-1, 0, -1), (1, 0, -1), (-1, 0, 1)])
    plane(m["yyzz"], m["yz"], m["yzz"], m["zyy"], [(0, 1, 1), (0, -1, -1), (0, 1, -1), (0, -1, 1)])
    sx = m["xx"] - (m["xxyy"] + m["xxzz"])
    sy = m["yy"] - (m["xxyy"] + m["yyzz"])
    sz = m["zz"] - (m["xxzz"] + m["yyzz"])
    dx = m["x"] - (m["xyy"] + m["xzz"])
    dy = m["y"] - (m["yxx"] + m["yzz"])
    dz = m["z"] - (m["zxx"] + m["zyy"])
    f[1], f[2] = 0.5 * (sx + dx), 0.5 * (sx - dx)
    f[3], f[4] = 0.5 * (sy + dy), 0.5 * (sy - dy)
    f[5], f[6] = 0.5 * (sz + dz), 0.5 * (sz - dz)
    f[0] = (m["1"] - (sx + sy)) - (sz + ((m["xxyy"] + m["xxzz"]) + m["yyzz"]))
    return f


NAMES = [
    "1", "x", "y", "z", "xy", "xz", "yz", "xx", "yy", "zz",
    "xyy", "xzz", "yxx", "yzz", "zxx", "zyy", "xxyy", "xxzz", "yyzz",
]


def collide(f, fluid, near, rates):
    third = 1.0 / 3.0
    m = to_moments(f)
    here = near(0, 0)
    xp, xm, yp, ym = near(1, 0), near(-1, 0), near(0, 1), near(0, -1)
    dx, dy = xp - xm, yp - ym
    ring = (2.0 * here + (xp + xm)) + (yp + ym)
    pp, pm, mp, mm = near(1, 1), near(1, -1), near(-1, 1), near(-1, -1)
    a, b = pp - mm, pm - mp
    scale = (COUPLING / 36.0) * here
    fx = scale * ((2.0 * dx + (a + b)) + (roll_z(dx, 1) + roll_z(dx, -1)))
    fy = scale * ((2.0 * dy + (a - b)) + (roll_z(dy, 1) + roll_z(dy, -1)))
    fz = scale * (roll_z(ring, -1) - roll_z(ring, 1))
    rho = jnp.where(fluid, m["1"], 1.0)
    inv = 1.0 / rho
    ux, uy, uz = ((m[n] + 0.5 * v) * inv for n, v in (("x", fx), ("y", fy), ("z", fz)))
    jx, jy, jz = rho * ux, rho * uy, rho * uz
    qx, qy, qz = jx * ux, jy * uy, jz * uz
    wx, wy, wz = ux * fx, uy * fy, uz * fz
    rho3, rho9 = rho * third, rho * (1.0 / 9.0)
    hx, hy, hz = (0.5 * q for q in (qx, qy, qz))
    hsum = rho9 - third * (hx + hy + hz)
    wsum = third * (wx + wy + wz)
    equil = {
        "1": rho, "x": jx, "y": jy, "z": jz,
        "xy": jx * uy, "xz": jx * uz, "yz": jy * uz,
        "xx": rho3 + qx, "yy": rho3 + qy, "zz": rho3 + qz,
        "xyy": jx * third, "yxx": jy * third, "zxx": jz * third,
        "xxyy": hsum + (hx + hy), "xxzz": hsum + (hx + hz), "yyzz": hsum + (hy + hz),
    }
    source = {
        "1": None, "x": fx, "y": fy, "z": fz,
        "xy": fx * uy + fy * ux, "xz": fx * uz + fz * ux, "yz": fy * uz + fz * uy,
        "xx": 2.0 * wx, "yy": 2.0 * wy, "zz": 2.0 * wz,
        "xyy": fx * third, "yxx": fy * third, "zxx": fz * third,
        "xxyy": (wx + wy) - wsum, "xxzz": (wx + wz) - wsum, "yyzz": (wy + wz) - wsum,
    }
    for table in (equil, source):
        table["xzz"], table["yzz"], table["zyy"] = table["xyy"], table["yxx"], table["zxx"]
    after = {}
    for row, name in enumerate(NAMES):
        rate = rates[row]
        if source[name] is None:
            after[name] = m[name] + rate * (equil[name] - m[name])
        else:
            after[name] = (m[name] + source[name]) + rate * (
                (equil[name] - m[name]) - 0.5 * source[name]
            )
    return from_moments(after), (ux, uy, uz)


def kernel(
    counts, pop_hbm, mask_hbm, wet_hbm, wall_hbm, rate_hbm, out_ref, vel_ref,
    pop_ref, mask_ref, wet_ref, wall_ref, rate_ref,
    pot, f_buf, dens, bits, post, pot_ysend, pot_yrecv, pot_crecv,
    xa_recv, ya_send, ya_recv, xb_send, xb_recv, yb_send, yb_recv, cb_send, cb_recv,
    ox, oy, gx_d, gy_d, y_tile,
    in_sem, pot_send_sem, pot_recv_sem, send_sem, recv_sem,
):
    nx, ny, nz = mask_ref.shape
    halves = ny // 8
    top = PAD + ny
    gx, gy = lax.axis_index("gx"), lax.axis_index("gy")
    SIGN = (-1, 1)
    leave_x, leave_y = (0, nx - 1), (0, ny - 1)
    enter_x, enter_y = (nx - 1, 0), (ny - 1, 0)
    ghost_x, ghost_y = (nx + 1, 0), (top, PAD - 1)
    XK = [ORDER[5:10], ORDER[0:5]]

    fetches = [
        pltpu.make_async_copy(a, b, in_sem.at[i])
        for i, (a, b) in enumerate(
            [
                (pop_hbm, pop_ref),
                (mask_hbm, mask_ref),
                (wet_hbm, wet_ref),
                (wall_hbm, wall_ref),
                (rate_hbm, rate_ref),
            ]
        )
    ]
    for copy in fetches:
        copy.start()

    def neighbour(d):
        return {
            "gx": lax.rem(gx + d[0] + counts[0], counts[0]),
            "gy": lax.rem(gy + d[1] + counts[1], counts[1]),
        }

    barrier = pltpu.get_barrier_semaphore()
    for d in SENDS:
        pl.semaphore_signal(
            barrier, inc=1, device_id=neighbour(d), device_id_type=pl.DeviceIdType.MESH
        )

    def remote(src, dst, sent, received, d):
        return pltpu.make_async_remote_copy(
            src_ref=src,
            dst_ref=dst,
            send_sem=sent,
            recv_sem=received,
            device_id=neighbour(d),
            device_id_type=pl.DeviceIdType.MESH,
        )

    rows = pl.ds(PAD, ny)
    xrows = pl.ds(PAD, nx)

    def pot_copies():
        pairs = {
            (1, 0): (pot.at[:, nx, rows], pot.at[:, 0, rows]),
            (-1, 0): (pot.at[:, 1, rows], pot.at[:, nx + 1, rows]),
        }
        for side, s in enumerate(SIGN):
            pairs[(0, s)] = (pot_ysend.at[side], pot_yrecv.at[side])
            for c, d in enumerate(CORNERS):
                if d[1] == s:
                    pairs[d] = (pot_ysend.at[side], pot_crecv.at[c])
        return [
            remote(*pairs[d], pot_send_sem.at[i], pot_recv_sem.at[i], d)
            for i, d in enumerate(SENDS)
        ]

    def a_copies(step):
        p = step % 2
        made = []
        for m, s in enumerate(SIGN):
            part = pl.ds(5 * (1 - m), 5)
            made.append(
                remote(
                    post.at[p, part, leave_x[m] + 1, rows], xa_recv.at[step, m, :, rows],
                    send_sem.at[step, m], recv_sem.at[step, m], (s, 0),
                )
            )
            made.append(
                remote(
                    ya_send.at[step, m, :, xrows], ya_recv.at[step, m, :, xrows],
                    send_sem.at[step, 2 + m], recv_sem.at[step, 2 + m], (0, s),
                )
            )
        return made

    def b_copies(step):
        made = []
        if step < STEPS - 1:
            for m, s in enumerate(SIGN):
                made.append(
                    remote(
                        xb_send.at[step, m], xb_recv.at[step, m],
                        send_sem.at[step, 4 + m], recv_sem.at[step, 4 + m], (s, 0),
                    )
                )
                made.append(
                    remote(
                        yb_send.at[step, m], yb_recv.at[step, m],
                        send_sem.at[step, 6 + m], recv_sem.at[step, 6 + m], (0, s),
                    )
                )
        for c, d in enumerate(CORNERS):
            made.append(
                remote(
                    cb_send.at[step, c], cb_recv.at[step, c],
                    send_sem.at[step, 8 + c], recv_sem.at[step, 8 + c], d,
                )
            )
        return made

    def clear():
        tile = jnp.zeros((8, nz), jnp.float32)
        for p in range(2):
            for m in range(2):
                for k in XK[m]:
                    for r in range((ny + 2 * PAD) // 8):
                        post[p, PLACE[k], ghost_x[m], pl.ds(8 * r, 8), :] = tile
                for k in CROSS[m]:
                    for x in range(nx):
                        post[p, PLACE[k], x + 1, pl.ds((top, 0)[m], 8), :] = tile
        for step in range(STEPS):
            for m in range(2):
                for j in range(5):
                    for r in (0, top):
                        xa_recv[step, m, j, pl.ds(r, 8), :] = tile
                    for r in (0, PAD + nx):
                        ya_send[step, m, j, pl.ds(r, 8), :] = tile
                        ya_recv[step, m, j, pl.ds(r, 8), :] = tile
                for r in range(halves):
                    xb_send[step, m, 1, pl.ds(8 * r, 8), :] = tile
                yb_send[step, m, 1] = jnp.zeros((nx, nz), jnp.float32)
            for c in range(4):
                cb_send[step, c] = tile

    def pot_unpack():
        for part in range(2):
            for m in range(2):
                for x in range(nx):
                    pot[part, x + 1, pl.ds(ghost_y[m], 1), :] = pot_yrecv[m, part, pl.ds(x, 1), :]
            for c, (sx, sy) in enumerate(CORNERS):
                mx, my = (sx + 1) // 2, (sy + 1) // 2
                pot[part, ghost_x[mx], pl.ds(ghost_y[my], 1), :] = pot_crecv[
                    c, part, pl.ds(leave_x[mx], 1), :
                ]

    def each_block(body):
        def plane(x, carry):
            for h in range(halves):
                body(x, h)
            return carry

        lax.fori_loop(0, nx, plane, 0)

    def first(x, h):
        block = pl.ds(8 * h, 8)
        fluid = mask_ref[x, block, :] == 1
        density = pop_ref[0, x, block, :]
        for k in range(1, 19):
            density = density + pop_ref[k, x, block, :]
        wet = wet_ref[x, block, :]
        wall = jnp.zeros_like(density)
        for c in range(WET_CLASSES):
            wall = wall + jnp.where(wet == c, wall_ref[c], 0.0)
        safe = jnp.where(fluid, density, 1.0)
        flag = jnp.where(fluid, 1.0, 0.0)
        for part, value in enumerate((jnp.where(fluid, 1.0 - jnp.exp(-safe), wall), flag)):
            pot[part, x + 1, pl.ds(PAD + 8 * h, 8), :] = value
            for m in range(2):
                if h == leave_y[m] // 8:
                    row = leave_y[m] % 8
                    pot_ysend[m, part, pl.ds(x, 1), :] = value[row : row + 1]

    def inflow(x, h):
        flags = jnp.zeros((8, nz), jnp.int32)
        for k, (ex, ey, ez) in enumerate(VEL):
            if k > 0:
                flag = roll_z(pot[1, x + 1 - ex, pl.ds(PAD + 8 * h - ey, 8), :], ez)
                flags = flags | jnp.where(flag == 1.0, 1 << k, 0)
        bits[x, pl.ds(8 * h, 8), :] = flags

    def collision(step, x, h):
        block = pl.ds(8 * h, 8)
        source = pop_ref if step == 0 else f_buf
        fluid = mask_ref[x, block, :] == 1
        near = lambda dx, dy: pot[0, x + 1 + dx, pl.ds(PAD + 8 * h + dy, 8), :]
        rates = [rate_ref[r] for r in range(19)]
        f, speed = collide([source[k, x, block, :] for k in range(19)], fluid, near, rates)
        for k in range(19):
            value = jnp.where(fluid, f[k], 0.0)
            post[step % 2, PLACE[k], x + 1, pl.ds(PAD + 8 * h, 8), :] = value
            for m in range(2):
                if k in CROSS[m] and h == leave_y[m] // 8:
                    row = leave_y[m] % 8
                    ya_send[step, m, CROSS[m].index(k), pl.ds(PAD + x, 1), :] = value[row : row + 1]
        if step == STEPS - 1:
            for c in range(3):
                vel_ref[c, x, block, :] = jnp.where(fluid, speed[c], 0.0)

    def stream(step, x, h):
        block, p = pl.ds(8 * h, 8), step % 2
        flags = bits[x, block, :]
        fluid = mask_ref[x, block, :] == 1
        density = None
        for k, (ex, ey, ez) in enumerate(VEL):
            if k == 0:
                value = post[p, PLACE[0], x + 1, pl.ds(PAD + 8 * h, 8), :]
            else:
                passed = roll_z(post[p, PLACE[k], x + 1 - ex, pl.ds(PAD + 8 * h - ey, 8), :], ez)
                bounced = post[p, PLACE[OPP[k]], x + 1, pl.ds(PAD + 8 * h, 8), :]
                value = jnp.where((flags & (1 << k)) != 0, passed, bounced)
            if step == STEPS - 1:
                out_ref[k, x, block, :] = jnp.where(fluid, value, 0.0)
            else:
                f_buf[k, x, block, :] = value
                density = value if density is None else density + value
        if step < STEPS - 1:
            dens[x, block, :] = density

    def edge_sums(step):
        p = step % 2
        for m in range(2):
            for h in range(halves):
                total = None
                for k in XK[m]:
                    _, ey, ez = VEL[k]
                    value = roll_z(
                        post[p, PLACE[k], leave_x[m] + 1, pl.ds(PAD + 8 * h - ey, 8), :], ez
                    )
                    total = value if total is None else total + value
                ox[m, pl.ds(8 * h, 8), :] = total
            total = None
            for j, k in enumerate(CROSS[m]):
                ex, _, ez = VEL[k]
                value = roll_z(ya_send[step, m, j, pl.ds(PAD - ex, nx), :], ez)
                total = value if total is None else total + value
            oy[m] = total

    def pack(step):
        one = lambda i: pl.ds(i, 1)
        for m in range(2):
            xb_send[step, m, 0] = dens[leave_x[m]]
            for n in range(2):
                xb_send[step, m, 1, one(n), :] = oy[n, one(leave_x[m]), :]
                yb_send[step, m, 1, one(n), :] = ox[n, one(leave_y[m]), :]
            for x in range(nx):
                yb_send[step, m, 0, one(x), :] = dens[x, one(leave_y[m]), :]
        for c, (sx, sy) in enumerate(CORNERS):
            mx, my = (sx + 1) // 2, (sy + 1) // 2
            cb_send[step, c, 1:2, :] = dens[leave_x[mx], one(leave_y[my]), :]
            cb_send[step, c, 2:3, :] = oy[my, one(leave_x[mx]), :]
            cb_send[step, c, 3:4, :] = ox[mx, one(leave_y[my]), :]

    def pack_corners(step):
        for c, (sx, sy) in enumerate(CORNERS):
            mx, my = (sx + 1) // 2, (sy + 1) // 2
            j = CROSS[my].index(INDEX[(sx, sy, 0)])
            cb_send[step, c, 0:1, :] = ya_send[step, my, j, pl.ds(PAD + leave_x[mx], 1), :]

    def arrive(step, k, x, block, value):
        if step == STEPS - 1:
            fluid = mask_ref[x, block, :] == 1
            out_ref[k, x, block, :] = out_ref[k, x, block, :] + jnp.where(fluid, value, 0.0)
        else:
            f_buf[k, x, block, :] = f_buf[k, x, block, :] + value

    def faces_arrive(step):
        inner = step < STEPS - 1
        for m in range(2):
            x = enter_x[m]
            for h in range(halves):
                block = pl.ds(8 * h, 8)
                total = None
                for j, k in enumerate(XK[m]):
                    _, ey, ez = VEL[k]
                    value = roll_z(xa_recv[step, m, j, pl.ds(PAD + 8 * h - ey, 8), :], ez)
                    arrive(step, k, x, block, value)
                    total = value if total is None else total + value
                if inner:
                    dens[x, block, :] = dens[x, block, :] + total
        for m in range(2):
            row = pl.ds(enter_y[m], 1)
            total = None
            for j, k in enumerate(CROSS[m]):
                ex, _, ez = VEL[k]
                value = roll_z(ya_recv[step, m, j, pl.ds(PAD - ex, nx), :], ez)
                y_tile[m, j] = value
                total = value if total is None else total + value
            y_tile[m, 5] = total
            for x in range(nx):
                for j, k in enumerate(CROSS[m]):
                    arrive(step, k, x, row, y_tile[m, j, pl.ds(x, 1), :])
                if inner:
                    dens[x, row, :] = dens[x, row, :] + y_tile[m, 5, pl.ds(x, 1), :]

    def own_potential(x, block, where):
        fluid = mask_ref[x, block, :] == 1
        value = 1.0 - jnp.exp(-dens[x, block, :])
        pot[0, x + 1, where, :] = jnp.where(fluid, value, pot[0, x + 1, where, :])

    def corners_arrive(step):
        for c, (sx, sy) in enumerate(CORNERS):
            mx, my = (sx + 1) // 2, (sy + 1) // 2
            x, y = enter_x[mx], enter_y[my]
            row = pl.ds(y, 1)
            value = cb_recv[step, c, 0:1, :]
            arrive(step, INDEX[(sx, sy, 0)], x, row, value)
            if step < STEPS - 1:
                dens[x, row, :] = dens[x, row, :] + value
                own_potential(x, row, pl.ds(PAD + y, 1))

    def ghost_potential(step):
        one = lambda i: pl.ds(i, 1)

        def put(x, where, density):
            flag = pot[1, x, where, :] == 1.0
            pot[0, x, where, :] = jnp.where(flag, 1.0 - jnp.exp(-density), pot[0, x, where, :])

        for m in range(2):
            gx_d[m] = xb_recv[step, m, 0] + ox[1 - m]
            gy_d[m] = yb_recv[step, m, 0] + oy[1 - m]
        for c, (sx, sy) in enumerate(CORNERS):
            mx, my = (sx + 1) // 2, (sy + 1) // 2
            x, y = enter_x[mx], enter_y[my]
            j = CROSS[my].index(INDEX[(-sx, sy, 0)])
            gx_d[mx, one(y), :] = gx_d[mx, one(y), :] + (
                ya_recv[step, my, j, one(PAD + x), :] + cb_recv[step, c, 2:3, :]
            )
            j = XK[mx].index(INDEX[(sx, -sy, 0)])
            gy_d[my, one(x), :] = gy_d[my, one(x), :] + (
                xa_recv[step, mx, j, one(PAD + y), :] + cb_recv[step, c, 3:4, :]
            )
            j = CROSS[1 - my].index(INDEX[(-sx, -sy, 0)])
            density = (
                cb_recv[step, c, 1:2, :] + ya_send[step, 1 - my, j, one(PAD + x), :]
            ) + (xb_recv[step, mx, 1, one(1 - my), :] + yb_recv[step, my, 1, one(1 - mx), :])
            put(ghost_x[mx], one(ghost_y[my]), density)
        for m in range(2):
            for h in range(halves):
                put(ghost_x[m], pl.ds(PAD + 8 * h, 8), gx_d[m, pl.ds(8 * h, 8), :])
            gy_d[m] = 1.0 - jnp.exp(-gy_d[m])
            for x in range(nx):
                where = one(ghost_y[m])
                flag = pot[1, x + 1, where, :] == 1.0
                pot[0, x + 1, where, :] = jnp.where(
                    flag, gy_d[m, one(x), :], pot[0, x + 1, where, :]
                )

    clear()
    for copy in fetches:
        copy.wait()
    each_block(first)
    pl.semaphore_wait(barrier, len(SENDS))
    moving = pot_copies()
    for copy in moving:
        copy.start()
    for copy in moving:
        copy.wait()
    pot_unpack()
    each_block(inflow)
    for step in range(STEPS):
        each_block(functools.partial(collision, step))
        faces = a_copies(step)
        for copy in faces:
            copy.start()
        pack_corners(step)
        others = b_copies(step)
        if step == STEPS - 1:
            for copy in others:
                copy.start()
            each_block(functools.partial(stream, step))
        else:
            each_block(functools.partial(stream, step))
            edge_sums(step)
            pack(step)
            for copy in others:
                copy.start()
        for copy in faces:
            copy.wait()
        faces_arrive(step)
        if step < STEPS - 1:
            each_block(
                lambda x, h: own_potential(x, pl.ds(8 * h, 8), pl.ds(PAD + 8 * h, 8))
            )
        for copy in others:
            copy.wait()
        corners_arrive(step)
        if step < STEPS - 1:
            ghost_potential(step)


def per_device(counts, populations, fluid_mask, wet_class, wall_potential, relax_rates):
    nx, ny, nz = fluid_mask.shape
    vmem = pl.BlockSpec(memory_space=pltpu.VMEM)
    hbm = pl.BlockSpec(memory_space=pltpu.HBM)
    f32 = jnp.float32
    padded = (nx + 2, ny + 2 * PAD, nz)
    return pl.pallas_call(
        functools.partial(kernel, counts),
        out_shape=(
            jax.ShapeDtypeStruct((19, nx, ny, nz), f32),
            jax.ShapeDtypeStruct((3, nx, ny, nz), f32),
        ),
        in_specs=[hbm] * 5,
        out_specs=(vmem, vmem),
        scratch_shapes=[
            pltpu.VMEM(populations.shape, f32),
            pltpu.VMEM(fluid_mask.shape, jnp.int32),
            pltpu.VMEM(wet_class.shape, jnp.int32),
            pltpu.SMEM(wall_potential.shape, f32),
            pltpu.SMEM(relax_rates.shape, f32),
            pltpu.VMEM((2,) + padded, f32),
            pltpu.VMEM((19, nx, ny, nz), f32),
            pltpu.VMEM((nx, ny, nz), f32),
            pltpu.VMEM((nx, ny, nz), jnp.int32),
            pltpu.VMEM((2, 19) + padded, f32),
            pltpu.VMEM((2, 2, nx, nz), f32),
            pltpu.VMEM((2, 2, nx, nz), f32),
            pltpu.VMEM((4, 2, nx, nz), f32),
            pltpu.VMEM((STEPS, 2, 5, ny + 2 * PAD, nz), f32),
            pltpu.VMEM((STEPS, 2, 5, nx + 2 * PAD, nz), f32),
            pltpu.VMEM((STEPS, 2, 5, nx + 2 * PAD, nz), f32),
            pltpu.VMEM((STEPS, 2, 2, ny, nz), f32),
            pltpu.VMEM((STEPS, 2, 2, ny, nz), f32),
            pltpu.VMEM((STEPS, 2, 2, nx, nz), f32),
            pltpu.VMEM((STEPS, 2, 2, nx, nz), f32),
            pltpu.VMEM((STEPS, 4, 8, nz), f32),
            pltpu.VMEM((STEPS, 4, 8, nz), f32),
            pltpu.VMEM((2, ny, nz), f32),
            pltpu.VMEM((2, nx, nz), f32),
            pltpu.VMEM((2, ny, nz), f32),
            pltpu.VMEM((2, nx, nz), f32),
            pltpu.VMEM((2, 6, nx, nz), f32),
            pltpu.SemaphoreType.DMA((5,)),
            pltpu.SemaphoreType.DMA((8,)),
            pltpu.SemaphoreType.DMA((8,)),
            pltpu.SemaphoreType.DMA((STEPS, 12)),
            pltpu.SemaphoreType.DMA((STEPS, 12)),
        ],
        compiler_params=pltpu.CompilerParams(
            collective_id=0, has_side_effects=True, vmem_limit_bytes=48 * 1024 * 1024
        ),
    )(populations, fluid_mask, wet_class, wall_potential, relax_rates)


def solution(mesh):
    counts = (mesh.shape["gx"], mesh.shape["gy"])
    return jax.shard_map(
        functools.partial(per_device, counts),
        mesh=mesh,
        in_specs=(
            P(None, ("groups", "gx"), "gy", None),
            P(("groups", "gx"), "gy", None),
            P(("groups", "gx"), "gy", None),
            P("groups"),
            P(),
        ),
        out_specs=(P(None, ("groups", "gx"), "gy", None), P(None, ("groups", "gx"), "gy", None)),
        check_vma=False,
    )
```

time: 58.9 us -> 45.7 us (0.78)
  Pallas kernels: 52 us -> 38.3 us
    pallas_call x1, Pallas kernels: 52 us -> 38.3 us  [per_device(): pl.pallas_call(functools.partial(kernel, counts), out_shape=(jax.ShapeDty...]
where the time goes in v2:
time: 45.7 us; the launch traced here: 45 us
  Pallas kernels  38.3 us (84%)
  local copies, waits for them, and re-layouts  5.99 us (13%)
  between operations  0.65 us (1%)
    pallas_call x1, Pallas kernels, per_device(): pl.pallas_call(functools.partial(kernel, counts), out_shape=(jax.ShapeDty...  38.3 us
    unnamed x12, local copies, waits for them, and re-layouts  5.99 us

profile of v2, /device:TPU:1, one launch (start us, length us, event | category | flops | bytes accessed | tf_op | source)
XLA Modules:
  0.0 45.0 jit_solution(1583308531614957311)
XLA Ops:
  0.6 0.0 copy-start
  0.6 1.3 %copy-done = f32[19,8,16,128]{3,2,1,0:T(8,128)S(1)} copy-done((f32[19,8,16,128]{3,2,1,0:T(8,128)S(1)}, f32[19,8,16,128]{3,2,1,0:T(8,128)}, u32[]{:S(2)}) %copy-start) | copy-done | bytes 1245208
  1.9 0.0 copy-start.1
  1.9 0.8 %copy-done.1 = s32[8,16,128]{2,1,0:T(8,128)S(1)} copy-done((s32[8,16,128]{2,1,0:T(8,128)S(1)}, s32[8,16,128]{2,1,0:T(8,128)}, u32[]{:S(2)}) %copy-start.1) | copy-done | bytes 65560
  2.8 0.0 copy-start.2
  2.8 0.8 %copy-done.2 = s32[8,16,128]{2,1,0:T(8,128)S(1)} copy-done((s32[8,16,128]{2,1,0:T(8,128)S(1)}, s32[8,16,128]{2,1,0:T(8,128)}, u32[]{:S(2)}) %copy-start.2) | copy-done | bytes 65560
  3.6 0.0 copy-start.3
  3.6 0.7 %copy-done.3 = f32[4]{0:T(128)S(1)} copy-done((f32[4]{0:T(128)S(1)}, f32[4]{0:T(128)}, u32[]{:S(2)}) %copy-start.3) | copy-done | bytes 40
  4.3 0.0 copy-start.4
  4.3 0.7 %copy-done.4 = f32[19]{0:T(128)S(1)} copy-done((f32[19]{0:T(128)S(1)}, f32[19]{0:T(128)}, u32[]{:S(2)}) %copy-start.4) | copy-done | bytes 100
  4.9 38.3 %shard_map.68 = (f32[19,8,16,128]{3,2,1,0:T(8,128)S(1)}, f32[3,8,16,128]{3,2,1,0:T(8,128)S(1)}) custom-call(f32[19,8,16,128]{3,2,1,0:T(8,128)S(1)} %copy-done, s32[8,16,128]{2,1,0:T(8,128)S(1)} %copy-done.1, s32[8,16,128]{2,1,0:T(8,128)S(1)} %copy-done.2, f32[4]{0:T(128)S(1)} %copy-done.3, f32[19]{0:T(128)S(1)} %copy-done.4), custom_call_target="tpu_custom_call" | custom-call | tf_op jit(solution)/shard_map/pallas_call | solution.py:570
  43.3 1.0 %copy.9 = f32[19,8,16,128]{3,2,1,0:T(8,128)} copy(f32[19,8,16,128]{3,2,1,0:T(8,128)S(1)} %get-tuple-element.4) | data formatting | bytes 2490368
  44.3 0.7 %copy.10 = f32[3,8,16,128]{3,2,1,0:T(8,128)} copy(f32[3,8,16,128]{3,2,1,0:T(8,128)S(1)} %get-tuple-element.5) | data formatting | bytes 393216
Async XLA Ops:
  0.6 1.3 %copy-start = (f32[19,8,16,128]{3,2,1,0:T(8,128)S(1)}, f32[19,8,16,128]{3,2,1,0:T(8,128)}, u32[]{:S(2)}) copy-start(f32[19,8,16,128]{3,2,1,0:T(8,128)} %pop_hbm.1) | copy-start | bytes 3735556
  1.9 0.8 %copy-start.1 = (s32[8,16,128]{2,1,0:T(8,128)S(1)}, s32[8,16,128]{2,1,0:T(8,128)}, u32[]{:S(2)}) copy-start(s32[8,16,128]{2,1,0:T(8,128)} %mask_hbm.1) | copy-start | bytes 196612
  2.8 0.8 %copy-start.2 = (s32[8,16,128]{2,1,0:T(8,128)S(1)}, s32[8,16,128]{2,1,0:T(8,128)}, u32[]{:S(2)}) copy-start(s32[8,16,128]{2,1,0:T(8,128)} %wet_hbm.1) | copy-start | bytes 196612
  3.6 0.7 %copy-start.3 = (f32[4]{0:T(128)S(1)}, f32[4]{0:T(128)}, u32[]{:S(2)}) copy-start(f32[4]{0:T(128)} %wall_hbm.1) | copy-start | bytes 52
  4.3 0.7 %copy-start.4 = (f32[19]{0:T(128)S(1)}, f32[19]{0:T(128)}, u32[]{:S(2)}) copy-start(f32[19]{0:T(128)} %rate_hbm.1) | copy-start | bytes 232

commit v3 on v2

--- a/solution.py
+++ b/solution.py
@@ -165,12 +165,12 @@
 
 
 def kernel(
-    counts, pop_hbm, mask_hbm, wet_hbm, wall_hbm, rate_hbm, out_ref, vel_ref,
-    pop_ref, mask_ref, wet_ref, wall_ref, rate_ref,
+    counts, pop_hbm, mask_hbm, wet_hbm, wall_hbm, rate_hbm, out_hbm, vel_hbm,
+    out_ref, vel_ref, pop_ref, mask_ref, wet_ref, wall_ref, rate_ref,
     pot, f_buf, dens, bits, post, pot_ysend, pot_yrecv, pot_crecv,
     xa_recv, ya_send, ya_recv, xb_send, xb_recv, yb_send, yb_recv, cb_send, cb_recv,
     ox, oy, gx_d, gy_d, y_tile,
-    in_sem, pot_send_sem, pot_recv_sem, send_sem, recv_sem,
+    in_sem, out_sem, pot_send_sem, pot_recv_sem, send_sem, recv_sem,
 ):
     nx, ny, nz = mask_ref.shape
     halves = ny // 8
@@ -237,48 +237,33 @@
             for i, d in enumerate(SENDS)
         ]
 
-    def a_copies(step):
+    def a_copies(step, dim):
         p = step % 2
         made = []
         for m, s in enumerate(SIGN):
-            part = pl.ds(5 * (1 - m), 5)
-            made.append(
-                remote(
-                    post.at[p, part, leave_x[m] + 1, rows], xa_recv.at[step, m, :, rows],
-                    send_sem.at[step, m], recv_sem.at[step, m], (s, 0),
-                )
-            )
-            made.append(
-                remote(
-                    ya_send.at[step, m, :, xrows], ya_recv.at[step, m, :, xrows],
-                    send_sem.at[step, 2 + m], recv_sem.at[step, 2 + m], (0, s),
-                )
-            )
+            if dim == "x":
+                part = pl.ds(5 * (1 - m), 5)
+                src = post.at[p, part, leave_x[m] + 1, rows]
+                dst, i, d = xa_recv.at[step, m, :, rows], m, (s, 0)
+            else:
+                src = ya_send.at[step, m, :, xrows]
+                dst, i, d = ya_recv.at[step, m, :, xrows], 2 + m, (0, s)
+            made.append(remote(src, dst, send_sem.at[step, i], recv_sem.at[step, i], d))
         return made
 
-    def b_copies(step):
+    def b_copies(step, dim):
         made = []
-        if step < STEPS - 1:
+        if dim == "corner":
+            for c, d in enumerate(CORNERS):
+                src, dst, i = cb_send.at[step, c], cb_recv.at[step, c], 8 + c
+                made.append(remote(src, dst, send_sem.at[step, i], recv_sem.at[step, i], d))
+        elif step < STEPS - 1:
             for m, s in enumerate(SIGN):
-                made.append(
-                    remote(
-                        xb_send.at[step, m], xb_recv.at[step, m],
-                        send_sem.at[step, 4 + m], recv_sem.at[step, 4 + m], (s, 0),
-                    )
-                )
-                made.append(
-                    remote(
-                        yb_send.at[step, m], yb_recv.at[step, m],
-                        send_sem.at[step, 6 + m], recv_sem.at[step, 6 + m], (0, s),
-                    )
-                )
-        for c, d in enumerate(CORNERS):
-            made.append(
-                remote(
-                    cb_send.at[step, c], cb_recv.at[step, c],
-                    send_sem.at[step, 8 + c], recv_sem.at[step, 8 + c], d,
-                )
-            )
+                if dim == "x":
+                    src, dst, i, d = xb_send.at[step, m], xb_recv.at[step, m], 4 + m, (s, 0)
+                else:
+                    src, dst, i, d = yb_send.at[step, m], yb_recv.at[step, m], 6 + m, (0, s)
+                made.append(remote(src, dst, send_sem.at[step, i], recv_sem.at[step, i], d))
         return made
 
     def clear():
@@ -296,11 +281,10 @@
                 for j in range(5):
                     for r in (0, top):
                         xa_recv[step, m, j, pl.ds(r, 8), :] = tile
+                    ya_send[step, m, j] = jnp.zeros((nx + 2 * PAD, nz), jnp.float32)
                     for r in (0, PAD + nx):
-                        ya_send[step, m, j, pl.ds(r, 8), :] = tile
                         ya_recv[step, m, j, pl.ds(r, 8), :] = tile
-                for r in range(halves):
-                    xb_send[step, m, 1, pl.ds(8 * r, 8), :] = tile
+                xb_send[step, m, pl.ds(ny, 8), :] = tile
                 yb_send[step, m, 1] = jnp.zeros((nx, nz), jnp.float32)
             for c in range(4):
                 cb_send[step, c] = tile
@@ -316,13 +300,13 @@
                     c, part, pl.ds(leave_x[mx], 1), :
                 ]
 
-    def each_block(body):
-        def plane(x, carry):
+    def each_block(body, start=0, count=nx, stride=1):
+        def plane(i, carry):
             for h in range(halves):
-                body(x, h)
+                body(start + i * stride, h)
             return carry
 
-        lax.fori_loop(0, nx, plane, 0)
+        lax.fori_loop(0, count, plane, 0)
 
     def first(x, h):
         block = pl.ds(8 * h, 8)
@@ -389,18 +373,20 @@
         if step < STEPS - 1:
             dens[x, block, :] = density
 
-    def edge_sums(step):
-        p = step % 2
+    def x_sums(step):
         for m in range(2):
             for h in range(halves):
                 total = None
                 for k in XK[m]:
                     _, ey, ez = VEL[k]
                     value = roll_z(
-                        post[p, PLACE[k], leave_x[m] + 1, pl.ds(PAD + 8 * h - ey, 8), :], ez
+                        post[step % 2, PLACE[k], leave_x[m] + 1, pl.ds(PAD + 8 * h - ey, 8), :], ez
                     )
                     total = value if total is None else total + value
                 ox[m, pl.ds(8 * h, 8), :] = total
+
+    def y_sums(step):
+        for m in range(2):
             total = None
             for j, k in enumerate(CROSS[m]):
                 ex, _, ez = VEL[k]
@@ -408,20 +394,25 @@
                 total = value if total is None else total + value
             oy[m] = total
 
-    def pack(step):
-        one = lambda i: pl.ds(i, 1)
-        for m in range(2):
-            xb_send[step, m, 0] = dens[leave_x[m]]
+    one = lambda i: pl.ds(i, 1)
+
+    def pack_x(step):
+        for m in range(2):
+            xb_send[step, m, pl.ds(0, ny), :] = dens[leave_x[m]]
             for n in range(2):
-                xb_send[step, m, 1, one(n), :] = oy[n, one(leave_x[m]), :]
-                yb_send[step, m, 1, one(n), :] = ox[n, one(leave_y[m]), :]
-            for x in range(nx):
-                yb_send[step, m, 0, one(x), :] = dens[x, one(leave_y[m]), :]
+                xb_send[step, m, one(ny + n), :] = oy[n, one(leave_x[m]), :]
         for c, (sx, sy) in enumerate(CORNERS):
             mx, my = (sx + 1) // 2, (sy + 1) // 2
             cb_send[step, c, 1:2, :] = dens[leave_x[mx], one(leave_y[my]), :]
             cb_send[step, c, 2:3, :] = oy[my, one(leave_x[mx]), :]
             cb_send[step, c, 3:4, :] = ox[mx, one(leave_y[my]), :]
+
+    def pack_y(step):
+        for m in range(2):
+            for n in range(2):
+                yb_send[step, m, 1, one(n), :] = ox[n, one(leave_y[m]), :]
+            for x in range(nx):
+                yb_send[step, m, 0, one(x), :] = dens[x, one(leave_y[m]), :]
 
     def pack_corners(step):
         for c, (sx, sy) in enumerate(CORNERS):
@@ -436,8 +427,7 @@
         else:
             f_buf[k, x, block, :] = f_buf[k, x, block, :] + value
 
-    def faces_arrive(step):
-        inner = step < STEPS - 1
+    def x_arrive(step):
         for m in range(2):
             x = enter_x[m]
             for h in range(halves):
@@ -448,8 +438,10 @@
                     value = roll_z(xa_recv[step, m, j, pl.ds(PAD + 8 * h - ey, 8), :], ez)
                     arrive(step, k, x, block, value)
                     total = value if total is None else total + value
-                if inner:
+                if step < STEPS - 1:
                     dens[x, block, :] = dens[x, block, :] + total
+
+    def y_arrive(step):
         for m in range(2):
             row = pl.ds(enter_y[m], 1)
             total = None
@@ -462,10 +454,11 @@
             for x in range(nx):
                 for j, k in enumerate(CROSS[m]):
                     arrive(step, k, x, row, y_tile[m, j, pl.ds(x, 1), :])
-                if inner:
+                if step < STEPS - 1:
                     dens[x, row, :] = dens[x, row, :] + y_tile[m, 5, pl.ds(x, 1), :]
 
-    def own_potential(x, block, where):
+    def own_potential(x, h):
+        block, where = pl.ds(8 * h, 8), pl.ds(PAD + 8 * h, 8)
         fluid = mask_ref[x, block, :] == 1
         value = 1.0 - jnp.exp(-dens[x, block, :])
         pot[0, x + 1, where, :] = jnp.where(fluid, value, pot[0, x + 1, where, :])
@@ -479,17 +472,14 @@
             arrive(step, INDEX[(sx, sy, 0)], x, row, value)
             if step < STEPS - 1:
                 dens[x, row, :] = dens[x, row, :] + value
-                own_potential(x, row, pl.ds(PAD + y, 1))
 
     def ghost_potential(step):
-        one = lambda i: pl.ds(i, 1)
-
         def put(x, where, density):
             flag = pot[1, x, where, :] == 1.0
             pot[0, x, where, :] = jnp.where(flag, 1.0 - jnp.exp(-density), pot[0, x, where, :])
 
         for m in range(2):
-            gx_d[m] = xb_recv[step, m, 0] + ox[1 - m]
+            gx_d[m] = xb_recv[step, m, pl.ds(0, ny), :] + ox[1 - m]
             gy_d[m] = yb_recv[step, m, 0] + oy[1 - m]
         for c, (sx, sy) in enumerate(CORNERS):
             mx, my = (sx + 1) // 2, (sy + 1) // 2
@@ -505,7 +495,7 @@
             j = CROSS[1 - my].index(INDEX[(-sx, -sy, 0)])
             density = (
                 cb_recv[step, c, 1:2, :] + ya_send[step, 1 - my, j, one(PAD + x), :]
-            ) + (xb_recv[step, mx, 1, one(1 - my), :] + yb_recv[step, my, 1, one(1 - mx), :])
+            ) + (xb_recv[step, mx, one(ny + 1 - my), :] + yb_recv[step, my, 1, one(1 - mx), :])
             put(ghost_x[mx], one(ghost_y[my]), density)
         for m in range(2):
             for h in range(halves):
@@ -530,40 +520,72 @@
         copy.wait()
     pot_unpack()
     each_block(inflow)
+
+    def start(group):
+        for copy in group:
+            copy.start()
+        return group
+
+    def finish(group):
+        for copy in group:
+            copy.wait()
+
+    EDGE, NEXT, INNER = (0, 2, nx - 1), (1, 2, nx - 3), (2, nx - 4, 1)
+    WITHIN = (1, nx - 2, 1)
     for step in range(STEPS):
-        each_block(functools.partial(collision, step))
-        faces = a_copies(step)
-        for copy in faces:
-            copy.start()
+        final = step == STEPS - 1
+        hit = functools.partial(collision, step)
+        move = functools.partial(stream, step)
+        each_block(hit, *EDGE)
+        x_moving = start(a_copies(step, "x"))
         pack_corners(step)
-        others = b_copies(step)
-        if step == STEPS - 1:
-            for copy in others:
-                copy.start()
-            each_block(functools.partial(stream, step))
+        if not final:
+            each_block(hit, *NEXT)
+            each_block(move, *EDGE)
+            x_sums(step)
+            y_sums(step)
+            pack_x(step)
+        x_moving += start(b_copies(step, "x") + b_copies(step, "corner"))
+        if final:
+            each_block(hit, *NEXT)
+        each_block(hit, *INNER)
+        y_moving = start(a_copies(step, "y"))
+        if final:
+            leaving = [pltpu.make_async_copy(vel_ref, vel_hbm, out_sem.at[0])]
+            leaving[0].start()
+            each_block(move)
         else:
-            each_block(functools.partial(stream, step))
-            edge_sums(step)
-            pack(step)
-            for copy in others:
-                copy.start()
-        for copy in faces:
-            copy.wait()
-        faces_arrive(step)
-        if step < STEPS - 1:
-            each_block(
-                lambda x, h: own_potential(x, pl.ds(8 * h, 8), pl.ds(PAD + 8 * h, 8))
-            )
-        for copy in others:
-            copy.wait()
+            each_block(move, *WITHIN)
+            y_sums(step)
+            pack_y(step)
+            y_moving += start(b_copies(step, "y"))
+        finish(y_moving)
+        y_arrive(step)
+        if final:
+            for i, (x, count) in enumerate([(1, nx - 2), (0, 1), (nx - 1, 1)]):
+                where = pl.ds(x, count)
+                leaving.append(
+                    pltpu.make_async_copy(
+                        out_ref.at[:, where], out_hbm.at[:, where], out_sem.at[1 + i]
+                    )
+                )
+            leaving[1].start()
+        else:
+            each_block(own_potential, *WITHIN)
+        finish(x_moving)
+        x_arrive(step)
         corners_arrive(step)
-        if step < STEPS - 1:
+        if final:
+            leaving[2].start()
+            leaving[3].start()
+            finish(leaving)
+        else:
+            each_block(own_potential, *EDGE)
             ghost_potential(step)
 
 
 def per_device(counts, populations, fluid_mask, wet_class, wall_potential, relax_rates):
     nx, ny, nz = fluid_mask.shape
-    vmem = pl.BlockSpec(memory_space=pltpu.VMEM)
     hbm = pl.BlockSpec(memory_space=pltpu.HBM)
     f32 = jnp.float32
     padded = (nx + 2, ny + 2 * PAD, nz)
@@ -574,8 +596,10 @@
             jax.ShapeDtypeStruct((3, nx, ny, nz), f32),
         ),
         in_specs=[hbm] * 5,
-        out_specs=(vmem, vmem),
+        out_specs=(hbm, hbm),
         scratch_shapes=[
+            pltpu.VMEM((19, nx, ny, nz), f32),
+            pltpu.VMEM((3, nx, ny, nz), f32),
             pltpu.VMEM(populations.shape, f32),
             pltpu.VMEM(fluid_mask.shape, jnp.int32),
             pltpu.VMEM(wet_class.shape, jnp.int32),
@@ -592,8 +616,8 @@
             pltpu.VMEM((STEPS, 2, 5, ny + 2 * PAD, nz), f32),
             pltpu.VMEM((STEPS, 2, 5, nx + 2 * PAD, nz), f32),
             pltpu.VMEM((STEPS, 2, 5, nx + 2 * PAD, nz), f32),
-            pltpu.VMEM((STEPS, 2, 2, ny, nz), f32),
-            pltpu.VMEM((STEPS, 2, 2, ny, nz), f32),
+            pltpu.VMEM((STEPS, 2, ny + 8, nz), f32),
+            pltpu.VMEM((STEPS, 2, ny + 8, nz), f32),
             pltpu.VMEM((STEPS, 2, 2, nx, nz), f32),
             pltpu.VMEM((STEPS, 2, 2, nx, nz), f32),
             pltpu.VMEM((STEPS, 4, 8, nz), f32),
@@ -604,13 +628,14 @@
             pltpu.VMEM((2, nx, nz), f32),
             pltpu.VMEM((2, 6, nx, nz), f32),
             pltpu.SemaphoreType.DMA((5,)),
+            pltpu.SemaphoreType.DMA((4,)),
             pltpu.SemaphoreType.DMA((8,)),
             pltpu.SemaphoreType.DMA((8,)),
             pltpu.SemaphoreType.DMA((STEPS, 12)),
             pltpu.SemaphoreType.DMA((STEPS, 12)),
         ],
         compiler_params=pltpu.CompilerParams(
-            collective_id=0, has_side_effects=True, vmem_limit_bytes=48 * 1024 * 1024
+            collective_id=0, has_side_effects=True, vmem_limit_bytes=60 * 1024 * 1024
         ),
     )(populations, fluid_mask, wet_class, wall_potential, relax_rates)
 

time: 45.7 us -> 39.5 us (0.86); the launches traced: 45 us -> 39.4 us
  local copies, waits for them, and re-layouts: 5.99 us -> 3.16 us
  Pallas kernels: 38.3 us -> 35.6 us
    unnamed x12 -> x4, local copies, waits for them, and re-layouts: 5.99 us -> 3.16 us
    pallas_call x1, Pallas kernels: 38.3 us -> 35.6 us  [per_device(): pl.pallas_call(functools.partial(kernel, counts), out_shape=(jax.ShapeDty...]
where the time goes in v3:
time: 39.5 us; the launch traced here: 39.4 us
  Pallas kernels  35.6 us (90%)
  local copies, waits for them, and re-layouts  3.16 us (8%)
  between operations  0.65 us (2%)
    pallas_call x1, Pallas kernels, per_device(): pl.pallas_call(functools.partial(kernel, counts), out_shape=(jax.ShapeDty...  35.6 us
    unnamed x4, local copies, waits for them, and re-layouts  3.16 us

profile of v3, /device:TPU:1, one launch (start us, length us, event | category | flops | bytes accessed | tf_op | source)
XLA Modules:
  0.0 39.4 jit_solution(1748876755852732584)
XLA Ops:
  0.6 35.6 %shard_map.68 = (f32[19,8,16,128]{3,2,1,0:T(8,128)}, f32[3,8,16,128]{3,2,1,0:T(8,128)}) custom-call(f32[19,8,16,128]{3,2,1,0:T(8,128)} %pop_hbm.1, s32[8,16,128]{2,1,0:T(8,128)} %mask_hbm.1, s32[8,16,128]{2,1,0:T(8,128)} %wet_hbm.1, f32[4]{0:T(128)} %wall_hbm.1, f32[19]{0:T(128)} %rate_hbm.1), custom_call_target="tpu_custom_call" | custom-call | tf_op jit(solution)/shard_map/pallas_call | solution.py:592
  36.2 0.0 copy-start
  36.2 2.5 %copy.9 = f32[19,8,16,128]{3,2,1,0:T(8,128)} copy(f32[19,8,16,128]{3,2,1,0:T(8,128)} %get-tuple-element.4) | data formatting | bytes 2490368
  38.7 0.0 copy-done
  38.7 0.7 %copy.10 = f32[3,8,16,128]{3,2,1,0:T(8,128)} copy(f32[3,8,16,128]{3,2,1,0:T(8,128)S(1)} %copy-done) | data formatting | bytes 393216
Async XLA Ops:
  36.2 2.5 %copy-start = (f32[3,8,16,128]{3,2,1,0:T(8,128)S(1)}, f32[3,8,16,128]{3,2,1,0:T(8,128)}, u32[]{:S(2)}) copy-start(f32[3,8,16,128]{3,2,1,0:T(8,128)} %get-tuple-element.5) | copy-start | bytes 589828
